TPU v7x, 128 devices: a whole 4x4x4 slice. The times are simulated.
128 devices in a mesh: row: 16 (over y, z), col: 8 (over x, core).
Axes of the slice: x: 4, y: 4, z: 4, core: 2. Of those that a mesh axis runs over, the one named last changes fastest.
Arguments:
- amplitudes: float32 [128, 512, 512], P(('row', 'col')), may hold values from -6 to 6
- integrals: float32 [512, 1024, 1024], P(('row', 'col')), may hold values from -0.01171875 to 0.01171875
- coupling: float32 [512, 32, 1024], P(('row', 'col')), may hold values from -0.046875 to 0.046875
- task_table: int32 [128, 4, 2], replicated, may hold values from -1 to 15, as said below
Outputs:
- residual: float32 [128, 1024], P(('row', 'col'))
Inputs may be any that keep to these rules, and one draw needn't show every extreme that they name: `task_table`: every virtual tile pair (C, D), C and D in 0 to 15, appears in exactly one slot. In each device's row the valid slots come first and the rest hold -1 in both entries. Some device has all 4 slots valid and some device has none. `integrals`: slots that task_table marks -1 are not read.
All inputs are finite; a program needn't handle non-finite values.
Results may differ from a plain program's by a relative error of at most 0.0003.
Values sent between devices are 32-bit elements; how exact they have to be, the bound alone decides.
No kernel may reach another device: no remote copies, remote signals or barrier semaphores. Data moves between devices by JAX's collectives and lax.ppermute only.
A program may use at most 128 MiB of HBM per device.

v0:
```python
import jax
import jax.numpy as jnp
from jax import lax
from jax.sharding import Mesh
from jax.sharding import PartitionSpec as P

TB = 32
NVT = 16
ROW = ("row_0", "row_1")
COL = ("col_0", "col_1")
ROW_COL = ("row_0", "row_1", "col_0", "col_1")


def split_up(value, dim, size):
    shape = value.shape
    tiles = value.reshape(*shape[:dim], size, shape[dim] // size, *shape[dim + 1 :])
    return jnp.moveaxis(tiles, dim, 0)


def sum_at_owner(value, axis, dim):
    size = lax.axis_size(axis)
    tiles = lax.all_to_all(split_up(value, dim, size), axis, 0, 0, tiled=True)
    return jnp.sum(tiles, axis=0)


def sum_by_axis(value, axes, dim):
    far, near = axes
    tiles = split_up(value, dim, lax.axis_size(far))
    nearer = sum_at_owner(tiles, near, dim + 1)
    arrived = lax.all_to_all(nearer, far, split_axis=0, concat_axis=0, tiled=True)
    return arrived.sum(axis=0)


def tile_stack(amplitudes):
    local_rows = amplitudes.shape[0]
    shaped = amplitudes.reshape(local_rows, NVT, TB, NVT, TB)
    return jnp.transpose(shaped, (1, 3, 0, 2, 4)).reshape(NVT * NVT, local_rows, TB * TB)


def body(amplitudes, integrals, coupling, task_table):
    row_count = lax.axis_size(ROW)
    col_count = lax.axis_size(COL)
    devices_all = row_count * col_count
    local_rows = amplitudes.shape[0]
    slot_total = integrals.shape[0]
    total_rows = devices_all * local_rows
    stacked = tile_stack(amplitudes)
    pair_ids = jnp.maximum(task_table[:, :, 0] * NVT + task_table[:, :, 1], 0).reshape(-1)
    outgoing = jnp.take(stacked, pair_ids, axis=0).reshape(
        devices_all, slot_total, local_rows, TB * TB
    )
    arrived = lax.all_to_all(outgoing, ROW_COL, split_axis=0, concat_axis=0, tiled=True)
    own_index = lax.axis_index(ROW_COL)
    own_tasks = lax.dynamic_index_in_dim(task_table, own_index, 0, keepdims=False)
    valid_count = jnp.sum((own_tasks[:, 0] >= 0).astype(jnp.int32))

    def add_tile(slot_index, partial_value):
        tile_rows = lax.dynamic_index_in_dim(arrived, slot_index, 1, keepdims=False).reshape(
            total_rows, TB * TB
        )
        integral_tile = lax.dynamic_index_in_dim(integrals, slot_index, 0, keepdims=False)
        product = lax.dot_general(
            tile_rows,
            integral_tile,
            (((1,), (1,)), ((), ())),
            precision=lax.Precision.HIGHEST,
            preferred_element_type=jnp.float32,
        )
        return partial_value + product

    ladder = lax.fori_loop(0, valid_count, add_tile, jnp.zeros((total_rows, TB * TB), jnp.float32))
    first_tile = amplitudes[:, :TB, :]
    pieces = lax.all_to_all(first_tile, ROW_COL, split_axis=2, concat_axis=0, tiled=True)
    width_part = pieces.shape[2]
    occupied = coupling.shape[1]
    window = total_rows // occupied
    regrouped = jnp.transpose(
        pieces.reshape(window, occupied, TB, width_part), (0, 2, 3, 1)
    ).reshape(window * TB, width_part * occupied)
    coupling_rows = coupling.reshape(width_part * occupied, occupied * TB)
    hole_term = jnp.dot(
        regrouped,
        coupling_rows,
        precision=lax.Precision.HIGHEST,
        preferred_element_type=jnp.float32,
    )
    hole_term = jnp.transpose(hole_term.reshape(window, TB, occupied, TB), (0, 2, 1, 3)).reshape(
        total_rows, TB * TB
    )
    return sum_by_axis(ladder + hole_term, (("row_0", "row_1", "col_0"), "col_1"), 0)


def solution(mesh):
    split = Mesh(mesh.devices.reshape(4, 4, 4, 2), ("row_0", "row_1", "col_0", "col_1"))
    in_specs = (P(ROW_COL, None, None), P(ROW_COL, None, None), P(ROW_COL, None, None), P())
    out_specs = P(ROW_COL, None)
    return jax.shard_map(body, mesh=split, in_specs=in_specs, out_specs=out_specs, check_vma=False)
```

profile of v0, /device:TPU:0, one launch (start us, length us, event | category | flops | bytes accessed | tf_op | source)
XLA Modules:
  0.0 128.8 jit_solution(13462357178927379148)
XLA Ops:
  0.0 0.9 slice.15
  1.1 0.5 broadcast.78
  1.6 1.2 reduce.3
  2.7 0.8 reshape.119
  3.5 11.1 %all-to-all-start.1 = ((f32[128,1,128]{2,1,0:T(1,128)}), f32[128,1,128]{2,1,0:T(1,128)S(1)}, u32[]{:S(2)}, u32[]{:S(2)}) async-start(f32[128,1,128]{2,1,0:T(1,128)} %reshape.119), calls=%async_computation.1 | async-start | bytes 131072 | tf_op jit(solution)/shard_map/all_to_all | solution.py:73
  14.7 2.5 %reshape.98 = f32[1,16,32,16,32]{4,3,2,1,0:T(8,128)} reshape(f32[1,512,512]{2,1,0:T(8,128)S(1)} %copy-done) | data formatting | bytes 2097152 | tf_op jit(solution)/shard_map/reshape | solution.py:36
  17.5 5.5 %copy.48 = f32[1,16,32,16,32]{4,2,3,1,0:T(8,128)} copy(f32[1,16,32,16,32]{4,3,2,1,0:T(8,128)} %reshape.98) | data formatting | bytes 2097152 | tf_op jit(solution)/shard_map/reshape | solution.py:36
  22.9 3.7 %reshape.103 = f32[256,1024]{1,0:T(8,128)S(1)} reshape(f32[16,16,1,32,32]{4,3,1,0,2:T(8,128)} %bitcast.49) | data formatting | bytes 2097152 | tf_op jit(solution)/shard_map/reshape | solution.py:37
  26.7 1.9 %gather_fusion = f32[512,1024]{1,0:T(8,128)S(1)} fusion(f32[256,1024]{1,0:T(8,128)S(1)} %reshape.103, s32[1024]{0:T(1024)S(1)} %pad_clamp_fusion), kind=kCustom, calls=%fused_computation | custom fusion | bytes 4196352 | tf_op jit(solution)/shard_map/jit(_take)/gather | solution.py:49
  28.6 3.6 %gather.11 = f32[128,4,1,1024]{3,2,1,0:T(1,128)} reshape(f32[512,1024]{1,0:T(8,128)S(1)} %gather_fusion) | data formatting | bytes 4194304 | tf_op jit(solution)/shard_map/jit(_take)/gather | solution.py:49
  32.2 0.1 copy.39
  32.3 4.8 %broadcast_select_fusion = f32[128,4,1,1024]{3,2,1,0:T(1,128)} fusion(f32[128,4,1,1024]{3,2,1,0:T(1,128)} %gather.11, pred[128,4]{1,0:T(8,128)(4,1)S(1)} %bitcast.55), kind=kLoop, calls=%fused_computation.10 | loop fusion | flops 524288 | bytes 4194816 | tf_op jit(solution)/shard_map/jit(_take)/select_n | solution.py:49
  37.1 9.9 %all-to-all-start = ((f32[128,4,1,1024]{3,2,1,0:T(1,128)}), f32[128,4,1,1024]{3,2,1,0:T(1,128)S(1)}, u32[]{:S(2)}, u32[]{:S(2)}) async-start(f32[128,4,1,1024]{3,2,1,0:T(1,128)} %broadcast_select_fusion), calls=%async_computation | async-start | bytes 4194304 | tf_op jit(solution)/shard_map/all_to_all | solution.py:52
  47.3 0.2 copy.36
  47.5 0.6 fusion.10
  48.1 0.7 reduce.4
  48.8 0.4 reshape.120
  49.3 0.2 copy.35
  49.4 0.2 reshape.116
  49.6 3.8 %convolution_bitcast_fusion = f32[4,32,32,32]{3,2,1,0:T(8,128)} fusion(f32[32,32,128,1]{2,1,0,3:T(8,128)S(1)} %bitcast.51, f32[4,32,128,1]{2,1,0,3:T(8,128)S(1)} %reshape.116), kind=kOutput, calls=%fused_computation.11 | convolution fusion | flops 201326592 | bytes 1114112 | tf_op jit(solution)/shard_map/dot_general | solution.py:81
  53.4 2.4 %reshape.102 = f32[128,1024]{1,0:T(8,128)S(1)} reshape(f32[4,32,32,32]{3,2,1,0:T(8,128)} %convolution_bitcast_fusion) | data formatting | bytes 1048576 | tf_op jit(solution)/shard_map/reshape | solution.py:87
  55.8 21.4 %all-to-all-done = f32[128,4,1,1024]{3,2,1,0:T(1,128)S(1)} async-done(((f32[128,4,1,1024]{3,2,1,0:T(1,128)}), f32[128,4,1,1024]{3,2,1,0:T(1,128)S(1)}, u32[]{:S(2)}, u32[]{:S(2)}) %all-to-all-start) | async-done | bytes 2097184 | tf_op jit(solution)/shard_map/all_to_all | solution.py:52
  77.3 22.8 %while.10 = (s32[]{:T(128)}, f32[128,1024]{1,0:T(8,128)S(1)}, s32[]{:T(128)}, f32[128,4,1,1024]{3,2,1,0:T(1,128)S(1)}, f32[4,1024,1024]{2,1,0:T(8,128)}, /*index=5*/s32[]{:T(128)}, s32[]{:T(128)}, s32[]{:T(128)}) while((s32[]{:T(128)}, f32[128,1024]{1,0:T(8,128)S(1)}, s32[]{:T(128)}, f32[128,4,1,1024]{3,2,1,0:T(1,128)S(1)}, ...), condition=%wide.region_2.3_spmd, body=%wide.region_1.2_spmd.sunk | while | flops 1610743808 | bytes 6815871 | solution.py:71
  78.0 6.7 %fusion.17 = f32[128,1024]{1,0:T(8,128)S(1)} fusion(f32[128,1024]{1,0:T(8,128)S(1)} %get-tuple-element.87, f32[4,1024,1024]{2,1,0:T(8,128)} %get-tuple-element.98, s32[]{:T(128)S(6)} %select_n.33, f32[128,1,1,1024]{3,2,1,0:T(1,128)S(1)} %constant_dynamic-slice_fusion.3), kind=kOutput, calls=%fused_computation.4.clone.1 | convolution fusion | flops 1610743808 | bytes 5767172 | tf_op jit(solution)/shard_map/while/body/dot_general | solution.py:62
  85.4 6.7 %fusion.17 = f32[128,1024]{1,0:T(8,128)S(1)} fusion(f32[128,1024]{1,0:T(8,128)S(1)} %get-tuple-element.87, f32[4,1024,1024]{2,1,0:T(8,128)} %get-tuple-element.98, s32[]{:T(128)S(6)} %select_n.33, f32[128,1,1,1024]{3,2,1,0:T(1,128)S(1)} %constant_dynamic-slice_fusion.3), kind=kOutput, calls=%fused_computation.4.clone.1 | convolution fusion | flops 1610743808 | bytes 5767172 | tf_op jit(solution)/shard_map/while/body/dot_general | solution.py:62
  92.8 6.7 %fusion.17 = f32[128,1024]{1,0:T(8,128)S(1)} fusion(f32[128,1024]{1,0:T(8,128)S(1)} %get-tuple-element.87, f32[4,1024,1024]{2,1,0:T(8,128)} %get-tuple-element.98, s32[]{:T(128)S(6)} %select_n.33, f32[128,1,1,1024]{3,2,1,0:T(1,128)S(1)} %constant_dynamic-slice_fusion.3), kind=kOutput, calls=%fused_computation.4.clone.1 | convolution fusion | flops 1610743808 | bytes 5767172 | tf_op jit(solution)/shard_map/while/body/dot_general | solution.py:62
  100.2 0.3 reshape_reshape.3
  100.5 0.2 copy.37
  100.7 10.6 %all_to_all.30 = f32[2,64,1,1024]{3,1,2,0:T(8,128)S(1)} all-to-all(f32[2,64,1,1024]{3,1,2,0:T(8,128)S(1)} %copy.37), channel_id=1, replica_groups=mesh['row_0'=4,'row_1'=4,'col_0'=4,'col_1'=2] {'col_1'}, dimensions={0} | all-to-all | bytes 1048576 | tf_op jit(solution)/shard_map/all_to_all | solution.py:22
  111.3 0.2 reduce_sum.33
  111.5 16.5 %all_to_all.31 = f32[64,1,1024]{2,1,0:T(1,128)S(1)} all-to-all(f32[64,1,1024]{2,1,0:T(1,128)S(1)} %reduce_sum.33), channel_id=1, replica_groups=mesh['row_0'=4,'row_1'=4,'col_0'=4,'col_1'=2] {'row_0','row_1','col_0'}, dimensions={0} | all-to-all | bytes 524288 | tf_op jit(solution)/shard_map/all_to_all | solution.py:30
  128.0 0.8 reduce_sum.34
  (20 shorter events, 0.9 us)
Async XLA Ops:
  0.0 14.7 %copy-start = (f32[1,512,512]{2,1,0:T(8,128)S(1)}, f32[1,512,512]{2,1,0:T(8,128)}, u32[]{:S(2)}) copy-start(f32[1,512,512]{2,1,0:T(8,128)} %param.6) | copy-start | bytes 3145732
  3.5 33.6 %all-to-all-start.1 = ((f32[128,1,128]{2,1,0:T(1,128)}), f32[128,1,128]{2,1,0:T(1,128)S(1)}, u32[]{:S(2)}, u32[]{:S(2)}) async-start(f32[128,1,128]{2,1,0:T(1,128)} %reshape.119), calls=%async_computation.1 | async-start | bytes 131072 | tf_op jit(solution)/shard_map/all_to_all | solution.py:73
  14.7 2.5 %copy-start.2 = (s32[128,4,2]{0,2,1:T(2,128)S(1)}, s32[128,4,2]{0,2,1:T(2,128)}, u32[]{:S(2)}) copy-start(s32[128,4,2]{0,2,1:T(2,128)} %param.9) | copy-start | bytes 12292
  37.1 10.1 %copy-start.1 = (f32[4,32,1024]{2,1,0:T(8,128)S(1)}, f32[4,32,1024]{2,1,0:T(8,128)}, u32[]{:S(2)}) copy-start(f32[4,32,1024]{2,1,0:T(8,128)} %param.8) | copy-start | bytes 1572868
  37.1 40.2 %all-to-all-start = ((f32[128,4,1,1024]{3,2,1,0:T(1,128)}), f32[128,4,1,1024]{3,2,1,0:T(1,128)S(1)}, u32[]{:S(2)}, u32[]{:S(2)}) async-start(f32[128,4,1,1024]{3,2,1,0:T(1,128)} %broadcast_select_fusion), calls=%async_computation | async-start | bytes 4194304 | tf_op jit(solution)/shard_map/all_to_all | solution.py:52
where the time goes:
time: 129 us
  blocking collectives  27.1 us (21%)
  local copies, waits for them, and re-layouts  24.4 us (19%)
  matrix products  23.8 us (18%)
  waiting for transfers between devices  21.4 us (17%)
  starting transfers between devices  21.1 us (16%)
  other arithmetic  8.22 us (6%)
  loops' own time  2.57 us (2%)
    all_to_all x1, waiting for transfers between devices, body(): lax.all_to_all(outgoing, ROW_COL, split_axis=0, concat_axis=0, tiled=True)  21.4 us
    dot_general x3, matrix products, add_tile(): lax.dot_general(tile_rows, integral_tile, (((1,), (1,)), ((), ())), preci...  20 us
    all_to_all x1, blocking collectives, sum_by_axis(): lax.all_to_all(nearer, far, split_axis=0, concat_axis=0, tiled=True)  16.5 us
    all_to_all x1, starting transfers between devices, body(): lax.all_to_all(first_tile, ROW_COL, split_axis=2, concat_axis=0, tiled=True)  11.1 us
    all_to_all x1, blocking collectives, sum_at_owner(): tiles = lax.all_to_all(split_up(value, dim, size), axis, 0, 0, tiled=True)  10.6 us
    all_to_all x1, starting transfers between devices, body(): lax.all_to_all(outgoing, ROW_COL, split_axis=0, concat_axis=0, tiled=True)  9.94 us
    reshape x2, local copies, waits for them, and re-layouts, tile_stack(): shaped = amplitudes.reshape(local_rows, NVT, TB, NVT, TB)  7.97 us
    gather x2, local copies, waits for them, and re-layouts, body(): jnp.take(stacked, pair_ids, axis=0)  5.48 us
  transfers between devices with their start and end apart: 2, of which 1 were waited for; matrix products, arithmetic and copies ran while one was open for 24% of the time, Pallas kernels for 0%

commit v1 on v0

v1 whole, which is shorter than its diff:
```python
import functools

import jax
import jax.numpy as jnp
from jax import lax
from jax.experimental import pallas as pl
from jax.experimental.pallas import tpu as pltpu
from jax.sharding import Mesh
from jax.sharding import PartitionSpec as P

TB = 32
NVT = 16
SLOTS = 4
DEVICES = 128
V = 512
PAIR = TB * TB
LANES = 128
MSG = SLOTS * 8 + 1
ROW_COL = ("row_0", "row_1", "col_0", "col_1")
F32 = jnp.float32
BF16 = jnp.bfloat16


def exchange_chunks(parts):
    lane = lax.broadcasted_iota(jnp.int32, parts[0].shape, parts[0].ndim - 1)
    odd = (lane // TB) % 2 == 1
    high = lane >= 2 * TB
    axis = parts[0].ndim - 1

    def swap(a, b, mask, shift):
        return (
            jnp.where(mask, pltpu.roll(b, shift, axis), a),
            jnp.where(mask, b, pltpu.roll(a, LANES - shift, axis)),
        )

    c0, c1 = swap(parts[0], parts[1], odd, TB)
    c2, c3 = swap(parts[2], parts[3], odd, TB)
    b0, b2 = swap(c0, c2, high, 2 * TB)
    b1, b3 = swap(c1, c3, high, 2 * TB)
    return b0, b1, b2, b3


def pack_kernel(table_ref, amp0_ref, amp1_ref, amp2_ref, amp3_ref, send_ref, stacked_ref, turned_ref):
    amp_refs = (amp0_ref, amp1_ref, amp2_ref, amp3_ref)

    def relayout(upper, _):
        row = pl.multiple_of(upper * TB, TB)
        for group in range(V // LANES):
            parts = [amp_refs[group][pl.ds(row + k, 8, stride=4), :] for k in range(4)]
            for h, tile in enumerate(exchange_chunks(parts)):
                stacked_ref[upper * NVT + group * 4 + h] = tile
        return 0

    lax.fori_loop(0, NVT, relayout, 0)

    def place(q, _):
        for s in range(SLOTS):
            pair = jnp.maximum(table_ref[s, 0, q] * NVT + table_ref[s, 1, q], 0)
            send_ref[pl.ds(q * MSG + s * 8, 8), :] = stacked_ref[pair]
        return 0

    lax.fori_loop(0, DEVICES, place, 0, unroll=4)
    for group in range(V // LANES):
        turned_ref[pl.ds(group * LANES, LANES), 0:TB] = amp_refs[group][0:TB, :].T
    parts = [turned_ref[pl.ds(k, DEVICES, stride=4), :] for k in range(4)]
    send_ref[pl.ds(SLOTS * 8, DEVICES, stride=MSG), :] = exchange_chunks(parts)[0]


def pack(table, amplitudes):
    return pl.pallas_call(
        pack_kernel,
        out_shape=jax.ShapeDtypeStruct((DEVICES * MSG, LANES), F32),
        in_specs=[
            pl.BlockSpec(memory_space=pltpu.SMEM),
            *[pl.BlockSpec((V, LANES), functools.partial(lambda g, _: (0, g), g)) for g in range(4)],
        ],
        grid=(1,),
        out_specs=pl.BlockSpec((DEVICES * MSG, LANES), lambda _: (0, 0)),
        scratch_shapes=[
            pltpu.VMEM((NVT * NVT, 8, LANES), F32),
            pltpu.VMEM((V, LANES), F32),
        ],
        compiler_params=pltpu.CompilerParams(vmem_limit_bytes=16 * 1024 * 1024),
        name="pack",
    )(table, *[amplitudes] * 4)


def split_parts(value):
    high = value.astype(BF16)
    return high, (value - high.astype(F32)).astype(BF16)


CHUNK = 256
CHUNKS = PAIR // CHUNK


def split_kernel(count_ref, int_ref, high_ref, low_ref):
    slot = pl.program_id(0)

    @pl.when(slot < count_ref[0])
    def _():
        high, low = split_parts(int_ref[...])
        high_ref[...] = high
        low_ref[...] = low


def split_integrals(count, integrals):
    def place(slot, chunk, count_ref):
        used = slot < count_ref[0]
        last = jnp.maximum(count_ref[0] - 1, 0)
        return jnp.where(used, slot, last), jnp.where(used, chunk, CHUNKS - 1), 0

    spec = pl.BlockSpec((1, CHUNK, PAIR), place)
    shape = jax.ShapeDtypeStruct((SLOTS, PAIR, PAIR), BF16)
    return pl.pallas_call(
        split_kernel,
        out_shape=(shape, shape),
        grid_spec=pltpu.PrefetchScalarGridSpec(
            num_scalar_prefetch=1, grid=(SLOTS, CHUNKS), in_specs=[spec], out_specs=[spec, spec]
        ),
        compiler_params=pltpu.CompilerParams(vmem_limit_bytes=16 * 1024 * 1024),
        cost_estimate=pl.CostEstimate(
            flops=SLOTS * PAIR * PAIR, bytes_accessed=SLOTS * PAIR * PAIR * 8, transcendentals=0
        ),
        name="split",
    )(count, integrals)


def nt_dot(a, b):
    return lax.dot_general(a, b, (((1,), (1,)), ((), ())), preferred_element_type=F32)


def tn_dot(a, b):
    return lax.dot_general(a, b, (((0,), (0,)), ((), ())), preferred_element_type=F32)


def main_kernel(count_ref, recv_ref, high_ref, low_ref, coup_ref, out_ref, both_ref, acc_ref, hole_ref):
    slot = pl.program_id(0)
    count = count_ref[0]

    @pl.when(slot == 0)
    def _():
        acc_ref[...] = jnp.zeros_like(acc_ref)

    @pl.when(slot < count)
    def _():
        for m in range(8):
            part = recv_ref[pl.ds(slot * 8 + m, DEVICES, stride=MSG), :]
            high, low = split_parts(part)
            both_ref[0:DEVICES, m * LANES : (m + 1) * LANES] = high
            both_ref[DEVICES:, m * LANES : (m + 1) * LANES] = low
        for chunk in range(CHUNKS):
            rows = slice(chunk * CHUNK, (chunk + 1) * CHUNK)
            top = nt_dot(both_ref[...], high_ref[0, rows, :])
            low = nt_dot(both_ref[0:DEVICES, :], low_ref[0, rows, :])
            acc_ref[:, rows] += top[:DEVICES] + top[DEVICES:] + low

    @pl.when(slot == SLOTS - 1)
    def _():
        data = recv_ref[pl.ds(SLOTS * 8, DEVICES, stride=MSG), :]
        blocks = exchange_chunks([data[i * TB : (i + 1) * TB] for i in range(4)])
        left_high, left_low = split_parts(jnp.concatenate(blocks, axis=0))
        right_high, right_low = split_parts(coup_ref[...])
        hole = tn_dot(left_high, right_high) + tn_dot(left_low, right_high) + tn_dot(left_high, right_low)
        for group in range(8):
            hole_ref[group] = hole[:, group * LANES : (group + 1) * LANES]
        for m in range(8):
            out_ref[pl.ds(m, DEVICES, stride=8), :] = acc_ref[:, m * LANES : (m + 1) * LANES]
        for i in range(4):
            for group in range(8):
                parts = [hole_ref[group, pl.ds(i * TB + k, 8, stride=4), :] for k in range(4)]
                for h, tile in enumerate(exchange_chunks(parts)):
                    row = (i * TB + group * 4 + h) * 8
                    out_ref[row : row + 8, :] += tile


def partial_residual(count, received, high, low, coupling):
    def place(slot, count_ref):
        return jnp.minimum(slot, jnp.maximum(count_ref[0] - 1, 0)), 0, 0

    spec = pl.BlockSpec((1, PAIR, PAIR), place)
    whole = lambda slot, count_ref: (0, 0)
    return pl.pallas_call(
        main_kernel,
        out_shape=jax.ShapeDtypeStruct((DEVICES * 8, LANES), F32),
        grid_spec=pltpu.PrefetchScalarGridSpec(
            num_scalar_prefetch=1,
            grid=(SLOTS,),
            in_specs=[
                pl.BlockSpec((DEVICES * MSG, LANES), whole),
                spec,
                spec,
                pl.BlockSpec((LANES, PAIR), whole),
            ],
            out_specs=pl.BlockSpec((DEVICES * 8, LANES), whole),
            scratch_shapes=[
                pltpu.VMEM((2 * DEVICES, PAIR), BF16),
                pltpu.VMEM((DEVICES, PAIR), F32),
                pltpu.VMEM((8, DEVICES, LANES), F32),
            ],
        ),
        compiler_params=pltpu.CompilerParams(vmem_limit_bytes=32 * 1024 * 1024),
        name="residual",
    )(count, received, high, low, coupling)


def body(amplitudes, integrals, coupling, task_table):
    table = jnp.transpose(task_table, (1, 2, 0))
    counts = jnp.sum((table[:, 0, :] >= 0).astype(jnp.int32), axis=0)
    count = lax.dynamic_slice(counts, (lax.axis_index(ROW_COL),), (1,))
    outgoing = pack(table, amplitudes.reshape(V, V))
    received = lax.all_to_all(
        outgoing.reshape(DEVICES, MSG, 1, LANES), ROW_COL, split_axis=0, concat_axis=0, tiled=True
    ).reshape(DEVICES * MSG, LANES)
    high, low = split_integrals(count, integrals)
    partial = partial_residual(count, received, high, low, coupling.reshape(LANES, PAIR))
    terms = lax.all_to_all(partial.reshape(DEVICES, 8, LANES), ROW_COL, split_axis=0, concat_axis=0, tiled=True)
    return jnp.sum(terms, axis=0).reshape(1, PAIR)


def solution(mesh):
    split = Mesh(mesh.devices.reshape(4, 4, 4, 2), ("row_0", "row_1", "col_0", "col_1"))
    in_specs = (P(ROW_COL, None, None), P(ROW_COL, None, None), P(ROW_COL, None, None), P())
    return jax.shard_map(body, mesh=split, in_specs=in_specs, out_specs=P(ROW_COL, None), check_vma=False)
```

time: 129 us -> 83.5 us (0.65)
  matrix products: 23.8 us -> 0 us
  starting transfers between devices: 21.1 us -> 11.1 us
  Pallas kernels: 0 us -> 9.25 us
  other arithmetic: 8.22 us -> 0.75 us
  blocking collectives: 27.1 us -> 22.4 us
  waiting for transfers between devices: 21.4 us -> 17.2 us
  local copies, waits for them, and re-layouts: 24.4 us -> 21.5 us
  loops' own time: 2.57 us -> 0 us
    dot_general x4 -> x0, matrix products: 23.8 us -> none  [the longest x3 20 us: add_tile(): lax.dot_general(tile_rows, integral_tile, (((1,), (1,)), ((), ())), preci...]
    unnamed x9 -> x18, local copies, waits for them, and re-layouts: 1.74 us -> 20.9 us
    reshape x4 -> x0, local copies, waits for them, and re-layouts: 14.1 us -> none  [the longest x2 7.97 us: tile_stack(): shaped = amplitudes.reshape(local_rows, NVT, TB, NVT, TB)]
    all_to_all x2 -> x1, starting transfers between devices: 21.1 us -> 11.1 us  [body(): lax.all_to_all(outgoing.reshape(DEVICES, MSG, 1, LANES), ROW_COL, split_a...]
    pallas_call x0 -> x3, Pallas kernels: none -> 9.25 us  [the longest x1 6.56 us: pack(): pl.pallas_call(pack_kernel, out_shape=jax.ShapeDtypeStruct((DEVICES * MSG...]
    gather x2 -> x0, local copies, waits for them, and re-layouts: 5.48 us -> none  [body(): jnp.take(stacked, pair_ids, axis=0)]
    select_n x1 -> x0, other arithmetic: 4.79 us -> none  [body(): jnp.take(stacked, pair_ids, axis=0)]
    all_to_all x2 -> x1, blocking collectives: 27.1 us -> 22.4 us  [body(): lax.all_to_all(partial.reshape(DEVICES, 8, LANES), ROW_COL, split_axis=0,...]
  transfers between devices with their start and end apart: 2 -> 1, of which waited for: 1 -> 1; matrix products, arithmetic and copies ran while one was open for 24% -> 1% of each run, Pallas kernels for 0% -> 1%
where the time goes in v1:
time: 83.5 us; the launch traced here: 82.3 us
  blocking collectives  22.4 us (27%)
  local copies, waits for them, and re-layouts  21.5 us (26%)
  waiting for transfers between devices  17.2 us (21%)
  starting transfers between devices  11.1 us (13%)
  Pallas kernels  9.25 us (11%)
    all_to_all x1, blocking collectives, body(): lax.all_to_all(partial.reshape(DEVICES, 8, LANES), ROW_COL, split_axis=0,...  22.4 us
    unnamed x18, local copies, waits for them, and re-layouts  20.9 us
    all_to_all x1, waiting for transfers between devices, body(): lax.all_to_all(outgoing.reshape(DEVICES, MSG, 1, LANES), ROW_COL, split_a...  17.2 us
    all_to_all x1, starting transfers between devices, body(): lax.all_to_all(outgoing.reshape(DEVICES, MSG, 1, LANES), ROW_COL, split_a...  11.1 us
    pallas_call x1, Pallas kernels, pack(): pl.pallas_call(pack_kernel, out_shape=jax.ShapeDtypeStruct((DEVICES * MSG...  6.56 us
  transfers between devices with their start and end apart: 1, of which 1 were waited for; matrix products, arithmetic and copies ran while one was open for 1% of the time, Pallas kernels for 1%

profile of v1, /device:TPU:0, one launch (start us, length us, event | category | flops | bytes accessed | tf_op | source)
XLA Modules:
  0.0 82.3 jit_solution(2550037458812444797)
XLA Ops:
  0.0 0.0 copy-start.1
  0.0 1.2 %copy-done.1 = f32[1,512,512]{2,1,0:T(8,128)S(1)} copy-done((f32[1,512,512]{2,1,0:T(8,128)S(1)}, f32[1,512,512]{2,1,0:T(8,128)}, u32[]{:S(2)}) %copy-start.1) | copy-done | bytes 1048600
  1.2 0.0 copy-start.7
  1.2 0.7 copy-done.7
  1.9 0.0 copy-start.8
  1.9 6.6 %pack.1 = f32[4224,128]{1,0:T(8,128)} custom-call(s32[4,2,128]{2,1,0:T(2,128)S(1)} %bitcast.14, f32[512,512]{1,0:T(8,128)S(1)} %bitcast.7, f32[512,512]{1,0:T(8,128)S(1)} %bitcast.8, f32[512,512]{1,0:T(8,128)S(1)} %bitcast.9, f32[512,512]{1,0:T(8,128)S(1)} %bitcast.10), custom_call_target="tpu_custom_call" | custom-call | tf_op jit(solution)/shard_map/pack/pallas_call | solution.py:70
  8.5 11.1 %all-to-all-start = ((f32[128,33,1,128]{3,2,1,0:T(1,128)}), f32[128,33,1,128]{3,2,1,0:T(1,128)S(1)}, u32[]{:S(2)}, u32[]{:S(2)}) async-start(f32[128,33,1,128]{3,2,1,0:T(1,128)} %bitcast.2), calls=%async_computation | async-start | bytes 4325376 | tf_op jit(solution)/shard_map/all_to_all | solution.py:212
  19.6 0.0 copy-done.8
  19.7 0.6 dynamic_slice.3.count_ref
  20.3 0.0 copy-start
  20.3 5.8 %copy-done = f32[4,1024,1024]{2,1,0:T(8,128)S(1)} copy-done((f32[4,1024,1024]{2,1,0:T(8,128)S(1)}, f32[4,1024,1024]{2,1,0:T(8,128)}, u32[]{:S(2)}) %copy-start) | copy-done | bytes 16777240
  26.0 0.0 copy-start.6
  26.0 1.0 %split.1 = (bf16[4,1024,1024]{2,1,0:T(8,128)(2,1)S(1)}, bf16[4,1024,1024]{2,1,0:T(8,128)(2,1)S(1)}) custom-call(s32[1]{0:T(128)} %dynamic_slice.3.count_ref, f32[4,1024,1024]{2,1,0:T(8,128)S(1)} %copy-done), custom_call_target="tpu_custom_call" | custom-call | flops 4194304 | bytes 33554432 | tf_op jit(solution)/shard_map/split/pallas_call | solution.py:115
  27.1 0.0 copy-start.2
  27.1 3.2 %copy-done.2 = bf16[4,1024,1024]{2,1,0:T(8,128)(2,1)} copy-done((bf16[4,1024,1024]{2,1,0:T(8,128)(2,1)}, bf16[4,1024,1024]{2,1,0:T(8,128)(2,1)S(1)}, u32[]{:S(2)}) %copy-start.2) | copy-done | bytes 8388632
  30.3 0.0 copy-start.4
  30.3 3.2 %copy-done.4 = bf16[4,1024,1024]{2,1,0:T(8,128)(2,1)} copy-done((bf16[4,1024,1024]{2,1,0:T(8,128)(2,1)}, bf16[4,1024,1024]{2,1,0:T(8,128)(2,1)S(1)}, u32[]{:S(2)}) %copy-start.4) | copy-done | bytes 8388632
  33.5 17.2 %all-to-all-done = f32[128,33,1,128]{3,2,1,0:T(1,128)S(1)} async-done(((f32[128,33,1,128]{3,2,1,0:T(1,128)}), f32[128,33,1,128]{3,2,1,0:T(1,128)S(1)}, u32[]{:S(2)}, u32[]{:S(2)}) %all-to-all-start) | async-done | bytes 2162720 | tf_op jit(solution)/shard_map/all_to_all | solution.py:212
  50.7 0.0 copy-done.6
  50.7 0.0 copy-start.3
  50.7 3.4 %copy-done.3 = bf16[4,1024,1024]{2,1,0:T(8,128)(2,1)S(1)} copy-done((bf16[4,1024,1024]{2,1,0:T(8,128)(2,1)S(1)}, bf16[4,1024,1024]{2,1,0:T(8,128)(2,1)}, u32[]{:S(2)}) %copy-start.3) | copy-done | bytes 8388632
  54.1 0.0 copy-start.5
  54.1 3.4 %copy-done.5 = bf16[4,1024,1024]{2,1,0:T(8,128)(2,1)S(1)} copy-done((bf16[4,1024,1024]{2,1,0:T(8,128)(2,1)S(1)}, bf16[4,1024,1024]{2,1,0:T(8,128)(2,1)}, u32[]{:S(2)}) %copy-start.5) | copy-done | bytes 8388632
  57.5 1.7 %residual.1 = f32[1024,128]{1,0:T(8,128)S(1)} custom-call(s32[1]{0:T(128)} %dynamic_slice.3.count_ref, f32[4224,128]{1,0:T(8,128)S(1)} %bitcast.11, bf16[4,1024,1024]{2,1,0:T(8,128)(2,1)S(1)} %copy-done.3, bf16[4,1024,1024]{2,1,0:T(8,128)(2,1)S(1)} %copy-done.5, f32[128,1024]{1,0:T(8,128)S(1)} %bitcast.13), custom_call_target="tpu_custom_call" | custom-call | tf_op jit(solution)/shard_map/residual/pallas_call | solution.py:183
  59.1 22.4 %all_to_all.10 = f32[128,8,128]{2,1,0:T(8,128)S(1)} all-to-all(f32[128,8,128]{2,1,0:T(8,128)S(1)} %bitcast.12), channel_id=1, replica_groups=mesh['row_0'=4,'row_1'=4,'col_0'=4,'col_1'=2] {'row_0','row_1','col_0','..., dimensions={0} | all-to-all | bytes 1048576 | tf_op jit(solution)/shard_map/all_to_all | solution.py:217
  81.5 0.7 reduce_sum.19
  (1 shorter events, 0.0 us)
Async XLA Ops:
  0.0 1.2 %copy-start.1 = (f32[1,512,512]{2,1,0:T(8,128)S(1)}, f32[1,512,512]{2,1,0:T(8,128)}, u32[]{:S(2)}) copy-start(f32[1,512,512]{2,1,0:T(8,128)} %param.4) | copy-start | bytes 3145732
  1.2 0.7 copy-start.7
  1.9 17.7 %copy-start.8 = (s32[128,4,2]{0,2,1:T(2,128)S(1)}, s32[128,4,2]{0,2,1:T(2,128)}, u32[]{:S(2)}) copy-start(s32[128,4,2]{0,2,1:T(2,128)} %param.7) | copy-start | bytes 12292
  8.5 42.2 %all-to-all-start = ((f32[128,33,1,128]{3,2,1,0:T(1,128)}), f32[128,33,1,128]{3,2,1,0:T(1,128)S(1)}, u32[]{:S(2)}, u32[]{:S(2)}) async-start(f32[128,33,1,128]{3,2,1,0:T(1,128)} %bitcast.2), calls=%async_computation | async-start | bytes 4325376 | tf_op jit(solution)/shard_map/all_to_all | solution.py:212
  20.3 5.8 %copy-start = (f32[4,1024,1024]{2,1,0:T(8,128)S(1)}, f32[4,1024,1024]{2,1,0:T(8,128)}, u32[]{:S(2)}) copy-start(f32[4,1024,1024]{2,1,0:T(8,128)} %int_ref.1) | copy-start | bytes 50331652
  26.0 24.7 %copy-start.6 = (f32[4,32,1024]{2,1,0:T(8,128)S(1)}, f32[4,32,1024]{2,1,0:T(8,128)}, u32[]{:S(2)}) copy-start(f32[4,32,1024]{2,1,0:T(8,128)} %param.6) | copy-start | bytes 1572868
  27.1 3.2 %copy-start.2 = (bf16[4,1024,1024]{2,1,0:T(8,128)(2,1)}, bf16[4,1024,1024]{2,1,0:T(8,128)(2,1)S(1)}, u32[]{:S(2)}) copy-start(bf16[4,1024,1024]{2,1,0:T(8,128)(2,1)S(1)} %get-tuple-element.7.high_ref) | copy-start | bytes 25165828
  30.3 3.2 %copy-start.4 = (bf16[4,1024,1024]{2,1,0:T(8,128)(2,1)}, bf16[4,1024,1024]{2,1,0:T(8,128)(2,1)S(1)}, u32[]{:S(2)}) copy-start(bf16[4,1024,1024]{2,1,0:T(8,128)(2,1)S(1)} %get-tuple-element.8.low_ref) | copy-start | bytes 25165828
  50.7 3.4 %copy-start.3 = (bf16[4,1024,1024]{2,1,0:T(8,128)(2,1)S(1)}, bf16[4,1024,1024]{2,1,0:T(8,128)(2,1)}, u32[]{:S(2)}) copy-start(bf16[4,1024,1024]{2,1,0:T(8,128)(2,1)} %copy-done.2) | copy-start | bytes 25165828
  54.1 3.4 %copy-start.5 = (bf16[4,1024,1024]{2,1,0:T(8,128)(2,1)S(1)}, bf16[4,1024,1024]{2,1,0:T(8,128)(2,1)}, u32[]{:S(2)}) copy-start(bf16[4,1024,1024]{2,1,0:T(8,128)(2,1)} %copy-done.4) | copy-start | bytes 25165828

commit v2 on v1

v2 whole, which is shorter than its diff:
```python
import functools

import jax
import jax.numpy as jnp
from jax import lax
from jax.experimental import pallas as pl
from jax.experimental.pallas import tpu as pltpu
from jax.sharding import Mesh
from jax.sharding import PartitionSpec as P

TB = 32
NVT = 16
SLOTS = 4
DEVICES = 128
V = 512
PAIR = TB * TB
LANES = 128
MSG = SLOTS * 8 + 1
ROW_COL = ("row_0", "row_1", "col_0", "col_1")
F32 = jnp.float32
BF16 = jnp.bfloat16


def exchange_chunks(parts):
    lane = lax.broadcasted_iota(jnp.int32, parts[0].shape, parts[0].ndim - 1)
    odd = (lane // TB) % 2 == 1
    high = lane >= 2 * TB
    axis = parts[0].ndim - 1

    def swap(a, b, mask, shift):
        return (
            jnp.where(mask, pltpu.roll(b, shift, axis), a),
            jnp.where(mask, b, pltpu.roll(a, LANES - shift, axis)),
        )

    c0, c1 = swap(parts[0], parts[1], odd, TB)
    c2, c3 = swap(parts[2], parts[3], odd, TB)
    b0, b2 = swap(c0, c2, high, 2 * TB)
    b1, b3 = swap(c1, c3, high, 2 * TB)
    return b0, b1, b2, b3


QUARTERS = V // LANES
TILES = NVT * NVT


def pack_kernel(table_hbm, amp_hbm, send_ref, table_ref, row_ref, place_ref, amp_ref, turned_ref, sems):
    table_copy = pltpu.make_async_copy(table_hbm, table_ref, sems.at[QUARTERS])
    table_copy.start()
    copies = []
    for group in range(QUARTERS):
        lanes = pl.ds(group * LANES, LANES)
        copies.append(pltpu.make_async_copy(amp_hbm.at[:, lanes], amp_ref.at[group], sems.at[group]))
        copies[-1].start()
    table_copy.wait()
    sublane = lax.broadcasted_iota(jnp.int32, (8, DEVICES), 0)
    device = lax.broadcasted_iota(jnp.int32, (8, DEVICES), 1)
    tiles = lax.broadcasted_iota(jnp.int32, (TILES, DEVICES), 0)
    found = jnp.zeros((8, TILES), F32)
    for s in range(SLOTS):
        pair = table_ref[s, 0:1, :] * NVT + table_ref[s, 1:2, :]
        match = (tiles == pair).astype(F32).astype(BF16)
        found += nt_dot(jnp.where(sublane == 0, device, s).astype(F32).astype(BF16), match)
    row_ref[...] = (found[0:1] * MSG + found[1:2] * 8).astype(jnp.int32)
    row_copy = pltpu.make_async_copy(row_ref, place_ref, sems.at[QUARTERS])
    row_copy.start()
    copies[0].wait()
    row_copy.wait()
    for group in range(QUARTERS):
        if group:
            copies[group].wait()
        parts = [amp_ref[group, pl.ds(k, DEVICES, stride=4), :] for k in range(4)]
        for h, tiles in enumerate(exchange_chunks(parts)):
            for upper in range(NVT):
                row = place_ref[0, upper * NVT + group * 4 + h]
                send_ref[pl.ds(row, 8), :] = tiles[upper * 8 : (upper + 1) * 8]
        turned_ref[pl.ds(group * LANES, LANES), 0:TB] = amp_ref[group, 0:TB, :].T
    parts = [turned_ref[pl.ds(k, DEVICES, stride=4), :] for k in range(4)]
    send_ref[pl.ds(SLOTS * 8, DEVICES, stride=MSG), :] = exchange_chunks(parts)[0]


def pack(table, amplitudes):
    hbm = pl.BlockSpec(memory_space=pltpu.HBM)
    return pl.pallas_call(
        pack_kernel,
        out_shape=jax.ShapeDtypeStruct((DEVICES * MSG, LANES), F32),
        in_specs=[hbm, hbm],
        out_specs=pl.BlockSpec(memory_space=pltpu.VMEM),
        scratch_shapes=[
            pltpu.VMEM((SLOTS, 2, DEVICES), jnp.int32),
            pltpu.VMEM((1, TILES), jnp.int32),
            pltpu.SMEM((1, TILES), jnp.int32),
            pltpu.VMEM((QUARTERS, V, LANES), F32),
            pltpu.VMEM((V, LANES), F32),
            pltpu.SemaphoreType.DMA((QUARTERS + 1,)),
        ],
        compiler_params=pltpu.CompilerParams(vmem_limit_bytes=16 * 1024 * 1024),
        name="pack",
    )(
        pltpu.with_memory_space_constraint(table, pltpu.HBM),
        pltpu.with_memory_space_constraint(amplitudes, pltpu.HBM),
    )


def nt_dot(a, b):
    return lax.dot_general(a, b, (((1,), (1,)), ((), ())), preferred_element_type=F32)


def nn_dot(a, b):
    return lax.dot_general(a, b, (((1,), (0,)), ((), ())), preferred_element_type=F32)


def split_parts(value):
    high = value.astype(BF16)
    return high, (value - high.astype(F32)).astype(BF16)


PIECE = 256


def main_kernel(table_hbm, recv_ref, int_hbm, coup_ref, out_ref, table_ref, int_ref, both_ref, acc_ref, hole_ref, sems):
    def fetch(slot):
        return pltpu.make_async_copy(int_hbm.at[slot], int_ref.at[slot], sems.at[slot])

    fetch(0).start()
    table_copy = pltpu.make_async_copy(table_hbm, table_ref, sems.at[SLOTS])
    table_copy.start()
    data = recv_ref[pl.ds(SLOTS * 8, DEVICES, stride=MSG), :]
    blocks = exchange_chunks([data[i * TB : (i + 1) * TB] for i in range(4)])
    left_high, left_low = split_parts(jnp.concatenate(blocks, axis=0).T)
    right_high, right_low = split_parts(coup_ref[...])
    hole = nn_dot(left_high, right_high) + nn_dot(left_low, right_high) + nn_dot(left_high, right_low)
    for group in range(8):
        hole_ref[group] = hole[:, group * LANES : (group + 1) * LANES]
    for group in range(8):
        parts = [hole_ref[group, pl.ds(k, DEVICES // 4, stride=4), :] for k in range(4)]
        for h, tiles in enumerate(exchange_chunks(parts)):
            for i in range(4):
                row = (i * TB + group * 4 + h) * 8
                out_ref[row : row + 8, :] = tiles[i * 8 : (i + 1) * 8]

    table_copy.wait()
    own = lax.axis_index(ROW_COL)
    count = jnp.int32(0)
    for s in range(SLOTS):
        count += (table_ref[s, 0, own] >= 0).astype(jnp.int32)

    @pl.when(count > 1)
    def _():
        fetch(1).start()

    acc_ref[...] = jnp.zeros_like(acc_ref)

    def prepare(slot, _):
        for m in range(8):
            high, low = split_parts(recv_ref[pl.ds(slot * 8 + m, DEVICES, stride=MSG), :])
            both_ref[slot, 0:DEVICES, m * LANES : (m + 1) * LANES] = high
            both_ref[slot, DEVICES:, m * LANES : (m + 1) * LANES] = low
        return 0

    lax.fori_loop(0, count, prepare, 0)
    fetch(0).wait()

    def add_slot(slot, _):
        @pl.when(slot > 0)
        def _():
            fetch(slot).wait()

        @pl.when(slot + 2 < count)
        def _():
            fetch(slot + 2).start()

        for piece in range(PAIR // PIECE):
            rows = slice(piece * PIECE, (piece + 1) * PIECE)
            int_high, int_low = split_parts(int_ref[slot, rows, :])
            top = nt_dot(int_high, both_ref[slot])
            low = nt_dot(int_low, both_ref[slot, 0:DEVICES, :])
            acc_ref[rows, :] += top[:, :DEVICES] + top[:, DEVICES:] + low
        return 0

    lax.fori_loop(0, count, add_slot, 0)
    for m in range(8):
        out_ref[pl.ds(m, DEVICES, stride=8), :] += acc_ref[m * LANES : (m + 1) * LANES, :].T


def partial_residual(table, received, integrals, coupling):
    whole = pl.BlockSpec(memory_space=pltpu.VMEM)
    hbm = pl.BlockSpec(memory_space=pltpu.HBM)
    return pl.pallas_call(
        main_kernel,
        out_shape=jax.ShapeDtypeStruct((DEVICES * 8, LANES), F32),
        in_specs=[hbm, whole, hbm, whole],
        out_specs=whole,
        scratch_shapes=[
            pltpu.SMEM((SLOTS, 2, DEVICES), jnp.int32),
            pltpu.VMEM((SLOTS, PAIR, PAIR), F32),
            pltpu.VMEM((SLOTS, 2 * DEVICES, PAIR), BF16),
            pltpu.VMEM((PAIR, DEVICES), F32),
            pltpu.VMEM((8, DEVICES, LANES), F32),
            pltpu.SemaphoreType.DMA((SLOTS + 1,)),
        ],
        compiler_params=pltpu.CompilerParams(vmem_limit_bytes=40 * 1024 * 1024),
        name="residual",
    )(pltpu.with_memory_space_constraint(table, pltpu.HBM), received, pltpu.with_memory_space_constraint(integrals, pltpu.HBM), coupling)


def body(amplitudes, integrals, coupling, task_table):
    table = jnp.transpose(task_table, (1, 2, 0))
    outgoing = pack(table, amplitudes.reshape(V, V))
    received = lax.all_to_all(
        outgoing.reshape(DEVICES, MSG, 1, LANES), ROW_COL, split_axis=0, concat_axis=0, tiled=True
    ).reshape(DEVICES * MSG, LANES)
    partial = partial_residual(table, received, integrals, coupling.reshape(LANES, PAIR))
    terms = lax.all_to_all(partial.reshape(DEVICES, 8, LANES), ROW_COL, split_axis=0, concat_axis=0, tiled=True)
    return jnp.sum(terms, axis=0).reshape(1, PAIR)


def solution(mesh):
    split = Mesh(mesh.devices.reshape(4, 4, 4, 2), ("row_0", "row_1", "col_0", "col_1"))
    in_specs = (P(ROW_COL, None, None), P(ROW_COL, None, None), P(ROW_COL, None, None), P())
    return jax.shard_map(body, mesh=split, in_specs=in_specs, out_specs=P(ROW_COL, None), check_vma=False)
```

time: 83.5 us -> 71.2 us (0.85)
  blocking collectives: 22.4 us -> 63.1 us
  local copies, waits for them, and re-layouts: 21.5 us -> 0.01 us
  waiting for transfers between devices: 17.2 us -> 0 us
  starting transfers between devices: 11.1 us -> 0 us
  Pallas kernels: 9.25 us -> 6.42 us
    all_to_all x0 -> x1, blocking collectives: none -> 42 us  [body(): lax.all_to_all(outgoing.reshape(DEVICES, MSG, 1, LANES), ROW_COL, split_a...]
    unnamed x18 -> x2, local copies, waits for them, and re-layouts: 20.9 us -> 0.01 us
    all_to_all x1 -> x0, waiting for transfers between devices: 17.2 us -> none  [body(): lax.all_to_all(outgoing.reshape(DEVICES, MSG, 1, LANES), ROW_COL, split_a...]
    all_to_all x1 -> x0, starting transfers between devices: 11.1 us -> none  [body(): lax.all_to_all(outgoing.reshape(DEVICES, MSG, 1, LANES), ROW_COL, split_a...]
    pallas_call x1, Pallas kernels: 6.56 us -> 2.71 us  [pack(): pl.pallas_call(pack_kernel, out_shape=jax.ShapeDtypeStruct((DEVICES * MSG...]
    pallas_call x1, Pallas kernels: 1.65 us -> 3.71 us  [partial_residual(): pl.pallas_call(main_kernel, out_shape=jax.ShapeDtypeStruct((DEVICES * 8,...]
    all_to_all x1, blocking collectives: 22.4 us -> 21.1 us  [body(): lax.all_to_all(partial.reshape(DEVICES, 8, LANES), ROW_COL, split_axis=0,...]
    pallas_call x1 -> x0, Pallas kernels: 1.03 us -> none  [split_integrals(): pl.pallas_call(split_kernel, out_shape=(shape, shape), grid_spec=pltpu.Pr...]
  transfers between devices with their start and end apart: 1 -> 0, of which waited for: 1 -> 0; matrix products, arithmetic and copies ran while one was open for 1% -> 0% of each run, Pallas kernels for 1% -> 0%
where the time goes in v2:
time: 71.2 us; the launch traced here: 70.3 us
  blocking collectives  63.1 us (89%)
  Pallas kernels  6.42 us (9%)
  other arithmetic  0.73 us (1%)
    all_to_all x1, blocking collectives, body(): lax.all_to_all(outgoing.reshape(DEVICES, MSG, 1, LANES), ROW_COL, split_a...  42 us
    all_to_all x1, blocking collectives, body(): lax.all_to_all(partial.reshape(DEVICES, 8, LANES), ROW_COL, split_axis=0,...  21.1 us
    pallas_call x1, Pallas kernels, partial_residual(): pl.pallas_call(main_kernel, out_shape=jax.ShapeDtypeStruct((DEVICES * 8,...  3.71 us
    pallas_call x1, Pallas kernels, pack(): pl.pallas_call(pack_kernel, out_shape=jax.ShapeDtypeStruct((DEVICES * MSG...  2.71 us

profile of v2, /device:TPU:0, one launch (start us, length us, event | category | flops | bytes accessed | tf_op | source)
XLA Modules:
  0.0 70.3 jit_solution(14611898887126308308)
XLA Ops:
  0.0 2.7 %pack.1 = f32[4224,128]{1,0:T(8,128)S(1)} custom-call(s32[4,2,128]{2,1,0:T(2,128)} %bitcast.12, f32[512,512]{1,0:T(8,128)} %bitcast.11), custom_call_target="tpu_custom_call" | custom-call | tf_op jit(solution)/shard_map/pack/pallas_call | solution.py:84
  2.7 0.0 copy-start
  2.7 42.0 %all_to_all.10 = f32[128,33,1,128]{3,2,1,0:T(1,128)S(1)} all-to-all(f32[128,33,1,128]{3,2,1,0:T(1,128)S(1)} %bitcast.7), channel_id=1, replica_groups=mesh['row_0'=4,'row_1'=4,'col_0'=4,'col_1'=2] {'row_0','row_1','col_0','..., dimensions={0} | all-to-all | bytes 4325376 | tf_op jit(solution)/shard_map/all_to_all | solution.py:210
  44.8 0.0 copy-done
  44.8 3.7 %residual.1 = f32[1024,128]{1,0:T(8,128)S(1)} custom-call(s32[4,2,128]{2,1,0:T(2,128)} %bitcast.13, f32[4224,128]{1,0:T(8,128)S(1)} %bitcast.8, f32[4,1024,1024]{2,1,0:T(8,128)} %int_hbm.1, f32[128,1024]{1,0:T(8,128)S(1)} %bitcast.10), custom_call_target="tpu_custom_call" | custom-call | tf_op jit(solution)/shard_map/residual/pallas_call | solution.py:189
  48.5 21.1 %all_to_all.11 = f32[128,8,128]{2,1,0:T(8,128)S(1)} all-to-all(f32[128,8,128]{2,1,0:T(8,128)S(1)} %bitcast.9), channel_id=1, replica_groups=mesh['row_0'=4,'row_1'=4,'col_0'=4,'col_1'=2] {'row_0','row_1','col_0','..., dimensions={0} | all-to-all | bytes 1048576 | tf_op jit(solution)/shard_map/all_to_all | solution.py:214
  69.6 0.7 %reduce_sum.9 = f32[8,128]{1,0:T(8,128)} reduce(f32[128,8,128]{2,1,0:T(8,128)S(1)} %all_to_all.11, f32[]{:T(128)} %constant.0.clone.1), dimensions={0}, to_apply=%region_0.0 | reduce | flops 130048 | bytes 528388 | tf_op jit(solution)/shard_map/reduce_sum | solution.py:215
Async XLA Ops:
  2.7 42.1 %copy-start = (f32[4,32,1024]{2,1,0:T(8,128)S(1)}, f32[4,32,1024]{2,1,0:T(8,128)}, u32[]{:S(2)}) copy-start(f32[4,32,1024]{2,1,0:T(8,128)} %param.6) | copy-start | bytes 1572868

commit v3 on v2

--- a/solution.py
+++ b/solution.py
@@ -44,7 +44,10 @@
 TILES = NVT * NVT
 
 
-def pack_kernel(table_hbm, amp_hbm, send_ref, table_ref, row_ref, place_ref, amp_ref, turned_ref, sems):
+def pack_kernel(
+    table_hbm, amp_hbm, int_hbm, send_ref, head_ref, table_ref, row_ref, place_ref, amp_ref, turned_ref, sems
+):
+    head_copy = pltpu.make_async_copy(int_hbm.at[0], head_ref, sems.at[QUARTERS + 1])
     table_copy = pltpu.make_async_copy(table_hbm, table_ref, sems.at[QUARTERS])
     table_copy.start()
     copies = []
@@ -52,6 +55,7 @@
         lanes = pl.ds(group * LANES, LANES)
         copies.append(pltpu.make_async_copy(amp_hbm.at[:, lanes], amp_ref.at[group], sems.at[group]))
         copies[-1].start()
+    head_copy.start()
     table_copy.wait()
     sublane = lax.broadcasted_iota(jnp.int32, (8, DEVICES), 0)
     device = lax.broadcasted_iota(jnp.int32, (8, DEVICES), 1)
@@ -77,28 +81,33 @@
         turned_ref[pl.ds(group * LANES, LANES), 0:TB] = amp_ref[group, 0:TB, :].T
     parts = [turned_ref[pl.ds(k, DEVICES, stride=4), :] for k in range(4)]
     send_ref[pl.ds(SLOTS * 8, DEVICES, stride=MSG), :] = exchange_chunks(parts)[0]
-
-
-def pack(table, amplitudes):
+    head_copy.wait()
+
+
+def pack(table, amplitudes, integrals):
     hbm = pl.BlockSpec(memory_space=pltpu.HBM)
     return pl.pallas_call(
         pack_kernel,
-        out_shape=jax.ShapeDtypeStruct((DEVICES * MSG, LANES), F32),
-        in_specs=[hbm, hbm],
-        out_specs=pl.BlockSpec(memory_space=pltpu.VMEM),
+        out_shape=(
+            jax.ShapeDtypeStruct((DEVICES * MSG, LANES), F32),
+            jax.ShapeDtypeStruct((PAIR, PAIR), F32),
+        ),
+        in_specs=[hbm, hbm, hbm],
+        out_specs=(pl.BlockSpec(memory_space=pltpu.VMEM),) * 2,
         scratch_shapes=[
             pltpu.VMEM((SLOTS, 2, DEVICES), jnp.int32),
             pltpu.VMEM((1, TILES), jnp.int32),
             pltpu.SMEM((1, TILES), jnp.int32),
             pltpu.VMEM((QUARTERS, V, LANES), F32),
             pltpu.VMEM((V, LANES), F32),
-            pltpu.SemaphoreType.DMA((QUARTERS + 1,)),
+            pltpu.SemaphoreType.DMA((QUARTERS + 2,)),
         ],
         compiler_params=pltpu.CompilerParams(vmem_limit_bytes=16 * 1024 * 1024),
         name="pack",
     )(
         pltpu.with_memory_space_constraint(table, pltpu.HBM),
         pltpu.with_memory_space_constraint(amplitudes, pltpu.HBM),
+        pltpu.with_memory_space_constraint(integrals, pltpu.HBM),
     )
 
 
@@ -118,13 +127,53 @@
 PIECE = 256
 
 
-def main_kernel(table_hbm, recv_ref, int_hbm, coup_ref, out_ref, table_ref, int_ref, both_ref, acc_ref, hole_ref, sems):
-    def fetch(slot):
-        return pltpu.make_async_copy(int_hbm.at[slot], int_ref.at[slot], sems.at[slot])
-
-    fetch(0).start()
+def main_kernel(
+    table_hbm,
+    recv_ref,
+    head_ref,
+    int_hbm,
+    coup_ref,
+    out_ref,
+    table_ref,
+    int_ref,
+    both_ref,
+    acc_ref,
+    hole_ref,
+    sems,
+):
     table_copy = pltpu.make_async_copy(table_hbm, table_ref, sems.at[SLOTS])
     table_copy.start()
+
+    def fetch(slot):
+        return pltpu.make_async_copy(int_hbm.at[slot], int_ref.at[slot - 1], sems.at[slot])
+
+    fetch(1).start()
+
+    def prepare(slot):
+        for m in range(8):
+            high, low = split_parts(recv_ref[pl.ds(slot * 8 + m, DEVICES, stride=MSG), :])
+            both_ref[slot, 0:DEVICES, m * LANES : (m + 1) * LANES] = high
+            both_ref[slot, DEVICES:, m * LANES : (m + 1) * LANES] = low
+
+    def product(slot, values):
+        int_high, int_low = split_parts(values)
+        top = nt_dot(int_high, both_ref[slot])
+        low = nt_dot(int_low, both_ref[slot, 0:DEVICES, :])
+        return top[:, :DEVICES] + top[:, DEVICES:] + low
+
+    pieces = [slice(first, first + PIECE) for first in range(0, PAIR, PIECE)]
+    prepare(0)
+    table_copy.wait()
+    own = lax.axis_index(ROW_COL)
+    count = jnp.int32(0)
+    for s in range(SLOTS):
+        count += (table_ref[s, 0, own] >= 0).astype(jnp.int32)
+    for slot in range(2, SLOTS):
+
+        @pl.when(slot < count)
+        def _():
+            fetch(slot).start()
+
     data = recv_ref[pl.ds(SLOTS * 8, DEVICES, stride=MSG), :]
     blocks = exchange_chunks([data[i * TB : (i + 1) * TB] for i in range(4)])
     left_high, left_low = split_parts(jnp.concatenate(blocks, axis=0).T)
@@ -139,61 +188,37 @@
                 row = (i * TB + group * 4 + h) * 8
                 out_ref[row : row + 8, :] = tiles[i * 8 : (i + 1) * 8]
 
-    table_copy.wait()
-    own = lax.axis_index(ROW_COL)
-    count = jnp.int32(0)
-    for s in range(SLOTS):
-        count += (table_ref[s, 0, own] >= 0).astype(jnp.int32)
-
-    @pl.when(count > 1)
-    def _():
-        fetch(1).start()
-
-    acc_ref[...] = jnp.zeros_like(acc_ref)
-
-    def prepare(slot, _):
-        for m in range(8):
-            high, low = split_parts(recv_ref[pl.ds(slot * 8 + m, DEVICES, stride=MSG), :])
-            both_ref[slot, 0:DEVICES, m * LANES : (m + 1) * LANES] = high
-            both_ref[slot, DEVICES:, m * LANES : (m + 1) * LANES] = low
-        return 0
-
-    lax.fori_loop(0, count, prepare, 0)
-    fetch(0).wait()
+    for rows in pieces:
+        acc_ref[rows, :] = jnp.where(count > 0, product(0, head_ref[rows, :]), 0.0)
+    fetch(1).wait()
 
     def add_slot(slot, _):
-        @pl.when(slot > 0)
+        prepare(slot)
+
+        @pl.when(slot > 1)
         def _():
             fetch(slot).wait()
 
-        @pl.when(slot + 2 < count)
-        def _():
-            fetch(slot + 2).start()
-
-        for piece in range(PAIR // PIECE):
-            rows = slice(piece * PIECE, (piece + 1) * PIECE)
-            int_high, int_low = split_parts(int_ref[slot, rows, :])
-            top = nt_dot(int_high, both_ref[slot])
-            low = nt_dot(int_low, both_ref[slot, 0:DEVICES, :])
-            acc_ref[rows, :] += top[:, :DEVICES] + top[:, DEVICES:] + low
+        for rows in pieces:
+            acc_ref[rows, :] += product(slot, int_ref[slot - 1, rows, :])
         return 0
 
-    lax.fori_loop(0, count, add_slot, 0)
+    lax.fori_loop(1, count, add_slot, 0)
     for m in range(8):
         out_ref[pl.ds(m, DEVICES, stride=8), :] += acc_ref[m * LANES : (m + 1) * LANES, :].T
 
 
-def partial_residual(table, received, integrals, coupling):
+def partial_residual(table, received, head, integrals, coupling):
     whole = pl.BlockSpec(memory_space=pltpu.VMEM)
     hbm = pl.BlockSpec(memory_space=pltpu.HBM)
     return pl.pallas_call(
         main_kernel,
         out_shape=jax.ShapeDtypeStruct((DEVICES * 8, LANES), F32),
-        in_specs=[hbm, whole, hbm, whole],
+        in_specs=[hbm, whole, whole, hbm, whole],
         out_specs=whole,
         scratch_shapes=[
             pltpu.SMEM((SLOTS, 2, DEVICES), jnp.int32),
-            pltpu.VMEM((SLOTS, PAIR, PAIR), F32),
+            pltpu.VMEM((SLOTS - 1, PAIR, PAIR), F32),
             pltpu.VMEM((SLOTS, 2 * DEVICES, PAIR), BF16),
             pltpu.VMEM((PAIR, DEVICES), F32),
             pltpu.VMEM((8, DEVICES, LANES), F32),
@@ -201,16 +226,22 @@
         ],
         compiler_params=pltpu.CompilerParams(vmem_limit_bytes=40 * 1024 * 1024),
         name="residual",
-    )(pltpu.with_memory_space_constraint(table, pltpu.HBM), received, pltpu.with_memory_space_constraint(integrals, pltpu.HBM), coupling)
+    )(
+        pltpu.with_memory_space_constraint(table, pltpu.HBM),
+        received,
+        head,
+        pltpu.with_memory_space_constraint(integrals, pltpu.HBM),
+        coupling,
+    )
 
 
 def body(amplitudes, integrals, coupling, task_table):
     table = jnp.transpose(task_table, (1, 2, 0))
-    outgoing = pack(table, amplitudes.reshape(V, V))
+    outgoing, head = pack(table, amplitudes.reshape(V, V), integrals)
     received = lax.all_to_all(
         outgoing.reshape(DEVICES, MSG, 1, LANES), ROW_COL, split_axis=0, concat_axis=0, tiled=True
     ).reshape(DEVICES * MSG, LANES)
-    partial = partial_residual(table, received, integrals, coupling.reshape(LANES, PAIR))
+    partial = partial_residual(table, received, head, integrals, coupling.reshape(LANES, PAIR))
     terms = lax.all_to_all(partial.reshape(DEVICES, 8, LANES), ROW_COL, split_axis=0, concat_axis=0, tiled=True)
     return jnp.sum(terms, axis=0).reshape(1, PAIR)
 

time: 71.2 us -> 70.4 us (0.989)
  blocking collectives: 63.1 us -> 59.5 us
  Pallas kernels: 6.42 us -> 9.58 us
    all_to_all x1, blocking collectives: 21.1 us -> 17.5 us  [body(): lax.all_to_all(partial.reshape(DEVICES, 8, LANES), ROW_COL, split_axis=0,...]
    pallas_call x1, Pallas kernels: 3.71 us -> 6.86 us  [partial_residual(): pl.pallas_call(main_kernel, out_shape=jax.ShapeDtypeStruct((DEVICES * 8,...]
where the time goes in v3:
time: 70.4 us; the launch traced here: 69.9 us
  blocking collectives  59.5 us (85%)
  Pallas kernels  9.58 us (14%)
  other arithmetic  0.73 us (1%)
    all_to_all x1, blocking collectives, body(): lax.all_to_all(outgoing.reshape(DEVICES, MSG, 1, LANES), ROW_COL, split_a...  42 us
    all_to_all x1, blocking collectives, body(): lax.all_to_all(partial.reshape(DEVICES, 8, LANES), ROW_COL, split_axis=0,...  17.5 us
    pallas_call x1, Pallas kernels, partial_residual(): pl.pallas_call(main_kernel, out_shape=jax.ShapeDtypeStruct((DEVICES * 8,...  6.86 us
    pallas_call x1, Pallas kernels, pack(): pl.pallas_call(pack_kernel, out_shape=(jax.ShapeDtypeStruct((DEVICES * MS...  2.72 us

profile of v3, /device:TPU:0, one launch (start us, length us, event | category | flops | bytes accessed | tf_op | source)
XLA Modules:
  0.0 69.9 jit_solution(3868688147564342538)
XLA Ops:
  0.0 2.7 %pack.1 = (f32[4224,128]{1,0:T(8,128)S(1)}, f32[1024,1024]{1,0:T(8,128)S(1)}) custom-call(s32[4,2,128]{2,1,0:T(2,128)} %bitcast.12, f32[512,512]{1,0:T(8,128)} %bitcast.11, f32[4,1024,1024]{2,1,0:T(8,128)} %int_hbm.3), custom_call_target="tpu_custom_call" | custom-call | tf_op jit(solution)/shard_map/pack/pallas_call | solution.py:89
  2.7 0.0 copy-start
  2.7 42.0 %all_to_all.10 = f32[128,33,1,128]{3,2,1,0:T(1,128)S(1)} all-to-all(f32[128,33,1,128]{3,2,1,0:T(1,128)S(1)} %bitcast.8), channel_id=1, replica_groups=mesh['row_0'=4,'row_1'=4,'col_0'=4,'col_1'=2] {'row_0','row_1','col_0','..., dimensions={0} | all-to-all | bytes 4325376 | tf_op jit(solution)/shard_map/all_to_all | solution.py:241
  44.8 0.0 copy-done
  44.8 6.9 %residual.1 = f32[1024,128]{1,0:T(8,128)S(1)} custom-call(s32[4,2,128]{2,1,0:T(2,128)} %bitcast.13, f32[4224,128]{1,0:T(8,128)S(1)} %bitcast.7, f32[1024,1024]{1,0:T(8,128)S(1)} %get-tuple-element.8.head_ref, f32[4,1024,1024]{2,1,0:T(8,128)} %int_hbm.3, f32[128,1024]{1,0:T(8,128)S(1)} %bitcast.10), custom_call_target="tpu_custom_call" | custom-call | tf_op jit(solution)/shard_map/residual/pallas_call | solution.py:214
  51.6 17.5 %all_to_all.11 = f32[128,8,128]{2,1,0:T(8,128)S(1)} all-to-all(f32[128,8,128]{2,1,0:T(8,128)S(1)} %bitcast.9), channel_id=1, replica_groups=mesh['row_0'=4,'row_1'=4,'col_0'=4,'col_1'=2] {'row_0','row_1','col_0','..., dimensions={0} | all-to-all | bytes 1048576 | tf_op jit(solution)/shard_map/all_to_all | solution.py:245
  69.2 0.7 %reduce_sum.9 = f32[8,128]{1,0:T(8,128)} reduce(f32[128,8,128]{2,1,0:T(8,128)S(1)} %all_to_all.11, f32[]{:T(128)} %constant.0.clone.1), dimensions={0}, to_apply=%region_0.0 | reduce | flops 130048 | bytes 528388 | tf_op jit(solution)/shard_map/reduce_sum | solution.py:246
Async XLA Ops:
  2.7 42.1 %copy-start = (f32[4,32,1024]{2,1,0:T(8,128)S(1)}, f32[4,32,1024]{2,1,0:T(8,128)}, u32[]{:S(2)}) copy-start(f32[4,32,1024]{2,1,0:T(8,128)} %param.6) | copy-start | bytes 1572868

commit v4 on v3

--- a/solution.py
+++ b/solution.py
@@ -125,6 +125,7 @@
 
 
 PIECE = 256
+HALF = DEVICES // 2
 
 
 def main_kernel(
@@ -133,12 +134,14 @@
     head_ref,
     int_hbm,
     coup_ref,
-    out_ref,
+    own_ref,
+    other_ref,
     table_ref,
     int_ref,
     both_ref,
     acc_ref,
     hole_ref,
+    turned_ref,
     sems,
 ):
     table_copy = pltpu.make_async_copy(table_hbm, table_ref, sems.at[SLOTS])
@@ -148,12 +151,16 @@
         return pltpu.make_async_copy(int_hbm.at[slot], int_ref.at[slot - 1], sems.at[slot])
 
     fetch(1).start()
+    core = lax.axis_index("col_1")
 
     def prepare(slot):
         for m in range(8):
-            high, low = split_parts(recv_ref[pl.ds(slot * 8 + m, DEVICES, stride=MSG), :])
-            both_ref[slot, 0:DEVICES, m * LANES : (m + 1) * LANES] = high
-            both_ref[slot, DEVICES:, m * LANES : (m + 1) * LANES] = low
+            lanes = slice(m * LANES, (m + 1) * LANES)
+            for half, parity in enumerate((core, 1 - core)):
+                part = recv_ref[pl.ds(parity * MSG + slot * 8 + m, HALF, stride=2 * MSG), :]
+                high, low = split_parts(part)
+                both_ref[slot, half * HALF : (half + 1) * HALF, lanes] = high
+                both_ref[slot, DEVICES + half * HALF : DEVICES + (half + 1) * HALF, lanes] = low
 
     def product(slot, values):
         int_high, int_low = split_parts(values)
@@ -185,8 +192,9 @@
         parts = [hole_ref[group, pl.ds(k, DEVICES // 4, stride=4), :] for k in range(4)]
         for h, tiles in enumerate(exchange_chunks(parts)):
             for i in range(4):
-                row = (i * TB + group * 4 + h) * 8
-                out_ref[row : row + 8, :] = tiles[i * 8 : (i + 1) * 8]
+                row = (i * TB + group * 4 + h) // 2 * 8
+                half = h % 2 + core - 2 * (h % 2) * core
+                turned_ref[pl.ds(half * (HALF * 8) + row, 8), :] = tiles[i * 8 : (i + 1) * 8]
 
     for rows in pieces:
         acc_ref[rows, :] = jnp.where(count > 0, product(0, head_ref[rows, :]), 0.0)
@@ -205,7 +213,10 @@
 
     lax.fori_loop(1, count, add_slot, 0)
     for m in range(8):
-        out_ref[pl.ds(m, DEVICES, stride=8), :] += acc_ref[m * LANES : (m + 1) * LANES, :].T
+        ladder = acc_ref[m * LANES : (m + 1) * LANES, :].T
+        for half, out_ref in enumerate((own_ref, other_ref)):
+            hole = turned_ref[pl.ds(half * (HALF * 8) + m, HALF, stride=8), :]
+            out_ref[pl.ds(m, HALF, stride=8), :] = hole + ladder[half * HALF : (half + 1) * HALF]
 
 
 def partial_residual(table, received, head, integrals, coupling):
@@ -213,15 +224,16 @@
     hbm = pl.BlockSpec(memory_space=pltpu.HBM)
     return pl.pallas_call(
         main_kernel,
-        out_shape=jax.ShapeDtypeStruct((DEVICES * 8, LANES), F32),
+        out_shape=(jax.ShapeDtypeStruct((HALF * 8, LANES), F32),) * 2,
         in_specs=[hbm, whole, whole, hbm, whole],
-        out_specs=whole,
+        out_specs=(whole, whole),
         scratch_shapes=[
             pltpu.SMEM((SLOTS, 2, DEVICES), jnp.int32),
             pltpu.VMEM((SLOTS - 1, PAIR, PAIR), F32),
             pltpu.VMEM((SLOTS, 2 * DEVICES, PAIR), BF16),
             pltpu.VMEM((PAIR, DEVICES), F32),
             pltpu.VMEM((8, DEVICES, LANES), F32),
+            pltpu.VMEM((DEVICES * 8, LANES), F32),
             pltpu.SemaphoreType.DMA((SLOTS + 1,)),
         ],
         compiler_params=pltpu.CompilerParams(vmem_limit_bytes=40 * 1024 * 1024),
@@ -241,8 +253,10 @@
     received = lax.all_to_all(
         outgoing.reshape(DEVICES, MSG, 1, LANES), ROW_COL, split_axis=0, concat_axis=0, tiled=True
     ).reshape(DEVICES * MSG, LANES)
-    partial = partial_residual(table, received, head, integrals, coupling.reshape(LANES, PAIR))
-    terms = lax.all_to_all(partial.reshape(DEVICES, 8, LANES), ROW_COL, split_axis=0, concat_axis=0, tiled=True)
+    own, other = partial_residual(table, received, head, integrals, coupling.reshape(LANES, PAIR))
+    arrived = lax.ppermute(other, "col_1", [(0, 1), (1, 0)])
+    chip = (own + arrived).reshape(HALF, 8, LANES)
+    terms = lax.all_to_all(chip, ROW_COL[:3], split_axis=0, concat_axis=0, tiled=True)
     return jnp.sum(terms, axis=0).reshape(1, PAIR)
 
 

time: 70.4 us -> 69.4 us (0.986)
  Pallas kernels: 9.58 us -> 8.19 us
  waiting for transfers between devices: 0 us -> 1.16 us
  starting transfers between devices: 0 us -> 1.05 us
  blocking collectives: 59.5 us -> 58.5 us
    pallas_call x1, Pallas kernels: 6.86 us -> 5.47 us  [partial_residual(): pl.pallas_call(main_kernel, out_shape=(jax.ShapeDtypeStruct((HALF * 8, LA...]
    ppermute x0 -> x1, waiting for transfers between devices: none -> 1.16 us  [body(): arrived = lax.ppermute(other, 'col_1', [(0, 1), (1, 0)])]
    all_to_all x1, blocking collectives: 17.5 us -> 16.4 us  [body(): lax.all_to_all(chip, ROW_COL[:3], split_axis=0, concat_axis=0, tiled=True)]
    ppermute x0 -> x1, starting transfers between devices: none -> 1.05 us  [body(): arrived = lax.ppermute(other, 'col_1', [(0, 1), (1, 0)])]
  transfers between devices with their start and end apart: 0 -> 1, of which waited for: 0 -> 1; matrix products, arithmetic and copies ran while one was open for 0% -> 0% of each run, Pallas kernels for 0% -> 0%
where the time goes in v4:
time: 69.4 us; the launch traced here: 69.6 us
  blocking collectives  58.5 us (84%)
  Pallas kernels  8.19 us (12%)
  waiting for transfers between devices  1.16 us (2%)
  starting transfers between devices  1.05 us (2%)
  other arithmetic  0.7 us (1%)
    all_to_all x1, blocking collectives, body(): lax.all_to_all(outgoing.reshape(DEVICES, MSG, 1, LANES), ROW_COL, split_a...  42 us
    all_to_all x1, blocking collectives, body(): lax.all_to_all(chip, ROW_COL[:3], split_axis=0, concat_axis=0, tiled=True)  16.4 us
    pallas_call x1, Pallas kernels, partial_residual(): pl.pallas_call(main_kernel, out_shape=(jax.ShapeDtypeStruct((HALF * 8, LA...  5.47 us
    pallas_call x1, Pallas kernels, pack(): pl.pallas_call(pack_kernel, out_shape=(jax.ShapeDtypeStruct((DEVICES * MS...  2.72 us
  transfers between devices with their start and end apart: 1, of which 1 were waited for; matrix products, arithmetic and copies ran while one was open for 0% of the time, Pallas kernels for 0%

profile of v4, /device:TPU:0, one launch (start us, length us, event | category | flops | bytes accessed | tf_op | source)
XLA Modules:
  0.0 69.6 jit_solution(687444099959028231)
XLA Ops:
  0.0 2.7 %pack.1 = (f32[4224,128]{1,0:T(8,128)S(1)}, f32[1024,1024]{1,0:T(8,128)S(1)}) custom-call(s32[4,2,128]{2,1,0:T(2,128)} %bitcast.12, f32[512,512]{1,0:T(8,128)} %bitcast.11, f32[4,1024,1024]{2,1,0:T(8,128)} %int_hbm.3), custom_call_target="tpu_custom_call" | custom-call | tf_op jit(solution)/shard_map/pack/pallas_call | solution.py:89
  2.7 0.0 copy-start
  2.7 42.0 %all_to_all.10 = f32[128,33,1,128]{3,2,1,0:T(1,128)S(1)} all-to-all(f32[128,33,1,128]{3,2,1,0:T(1,128)S(1)} %bitcast.9), channel_id=1, replica_groups=mesh['row_0'=4,'row_1'=4,'col_0'=4,'col_1'=2] {'row_0','row_1','col_0','..., dimensions={0} | all-to-all | bytes 4325376 | tf_op jit(solution)/shard_map/all_to_all | solution.py:253
  44.8 0.0 copy-done
  44.8 5.5 %residual.1 = (f32[512,128]{1,0:T(8,128)S(1)}, f32[512,128]{1,0:T(8,128)S(1)}) custom-call(s32[4,2,128]{2,1,0:T(2,128)} %bitcast.13, f32[4224,128]{1,0:T(8,128)S(1)} %bitcast.8, f32[1024,1024]{1,0:T(8,128)S(1)} %get-tuple-element.10.head_ref, f32[4,1024,1024]{2,1,0:T(8,128)} %int_hbm.3, f32[128,1024]{1,0:T(8,128)S(1)} %bitcast.10), custom_call_target="tpu_custom_call" | custom-call | tf_op jit(solution)/shard_map/residual/pallas_call | solution.py:225
  50.3 1.0 %collective-permute-start = (f32[512,128]{1,0:T(8,128)S(1)}, f32[512,128]{1,0:T(8,128)S(1)}, u32[]{:S(2)}, u32[]{:S(2)}) collective-permute-start(f32[512,128]{1,0:T(8,128)S(1)} %get-tuple-element.12), channel_id=1, source_target_pairs={{0,1},{1,0},{2,3},{3,2},{4,5},{5,4},{6,7},{7,6},{8,9},{9,8},{10,11... | collective-permute-start | bytes 786440 | tf_op jit(solution)/shard_map/ppermute | solution.py:257
  51.3 1.2 %collective-permute-done = f32[512,128]{1,0:T(8,128)S(1)} collective-permute-done((f32[512,128]{1,0:T(8,128)S(1)}, f32[512,128]{1,0:T(8,128)S(1)}, u32[]{:S(2)}, u32[]{:S(2)}) %collective-permute-start) | collective-permute-done | bytes 262176 | tf_op jit(solution)/shard_map/ppermute | solution.py:257
  52.5 16.4 %all_to_all.11 = f32[64,8,128]{2,1,0:T(8,128)S(1)} all-to-all(f32[64,8,128]{2,1,0:T(8,128)S(1)} %add_bitcast_fusion), channel_id=1, replica_groups=mesh['row_0'=4,'row_1'=4,'col_0'=4,'col_1'=2] {'row_0','row_1','col_0'}, dimensions={0} | all-to-all | bytes 524288 | tf_op jit(solution)/shard_map/all_to_all | solution.py:259
  68.9 0.7 reduce_sum.9
  (1 shorter events, 0.0 us)
Async XLA Ops:
  2.7 42.1 %copy-start = (f32[4,32,1024]{2,1,0:T(8,128)S(1)}, f32[4,32,1024]{2,1,0:T(8,128)}, u32[]{:S(2)}) copy-start(f32[4,32,1024]{2,1,0:T(8,128)} %param.6) | copy-start | bytes 1572868
  50.3 2.2 %collective-permute-start = (f32[512,128]{1,0:T(8,128)S(1)}, f32[512,128]{1,0:T(8,128)S(1)}, u32[]{:S(2)}, u32[]{:S(2)}) collective-permute-start(f32[512,128]{1,0:T(8,128)S(1)} %get-tuple-element.12), channel_id=1, source_target_pairs={{0,1},{1,0},{2,3},{3,2},{4,5},{5,4},{6,7},{7,6},{8,9},{9,8},{10,11... | collective-permute-start | bytes 786440 | tf_op jit(solution)/shard_map/ppermute | solution.py:257

commit v5 on v4

--- a/solution.py
+++ b/solution.py
@@ -27,27 +27,35 @@
     high = lane >= 2 * TB
     axis = parts[0].ndim - 1
 
-    def swap(a, b, mask, shift):
+    def swap(a, b):
         return (
-            jnp.where(mask, pltpu.roll(b, shift, axis), a),
-            jnp.where(mask, b, pltpu.roll(a, LANES - shift, axis)),
+            jnp.where(odd, pltpu.roll(b, TB, axis), a),
+            jnp.where(odd, b, pltpu.roll(a, LANES - TB, axis)),
         )
 
-    c0, c1 = swap(parts[0], parts[1], odd, TB)
-    c2, c3 = swap(parts[2], parts[3], odd, TB)
-    b0, b2 = swap(c0, c2, high, 2 * TB)
-    b1, b3 = swap(c1, c3, high, 2 * TB)
+    def swap_halves(a, b):
+        moved = pltpu.roll(jnp.where(high, a, b), 2 * TB, axis)
+        return jnp.where(high, moved, a), jnp.where(high, b, moved)
+
+    c0, c1 = swap(parts[0], parts[1])
+    c2, c3 = swap(parts[2], parts[3])
+    b0, b2 = swap_halves(c0, c2)
+    b1, b3 = swap_halves(c1, c3)
     return b0, b1, b2, b3
 
 
 QUARTERS = V // LANES
 TILES = NVT * NVT
+EXTRA = 256
 
 
 def pack_kernel(
     table_hbm, amp_hbm, int_hbm, send_ref, head_ref, table_ref, row_ref, place_ref, amp_ref, turned_ref, sems
 ):
-    head_copy = pltpu.make_async_copy(int_hbm.at[0], head_ref, sems.at[QUARTERS + 1])
+    head_copies = [
+        pltpu.make_async_copy(int_hbm.at[0], head_ref.at[0:PAIR, :], sems.at[QUARTERS + 1]),
+        pltpu.make_async_copy(int_hbm.at[1, 0:EXTRA, :], head_ref.at[PAIR:, :], sems.at[QUARTERS + 2]),
+    ]
     table_copy = pltpu.make_async_copy(table_hbm, table_ref, sems.at[QUARTERS])
     table_copy.start()
     copies = []
@@ -55,7 +63,8 @@
         lanes = pl.ds(group * LANES, LANES)
         copies.append(pltpu.make_async_copy(amp_hbm.at[:, lanes], amp_ref.at[group], sems.at[group]))
         copies[-1].start()
-    head_copy.start()
+    for copy in head_copies:
+        copy.start()
     table_copy.wait()
     sublane = lax.broadcasted_iota(jnp.int32, (8, DEVICES), 0)
     device = lax.broadcasted_iota(jnp.int32, (8, DEVICES), 1)
@@ -81,7 +90,8 @@
         turned_ref[pl.ds(group * LANES, LANES), 0:TB] = amp_ref[group, 0:TB, :].T
     parts = [turned_ref[pl.ds(k, DEVICES, stride=4), :] for k in range(4)]
     send_ref[pl.ds(SLOTS * 8, DEVICES, stride=MSG), :] = exchange_chunks(parts)[0]
-    head_copy.wait()
+    for copy in head_copies:
+        copy.wait()
 
 
 def pack(table, amplitudes, integrals):
@@ -90,7 +100,7 @@
         pack_kernel,
         out_shape=(
             jax.ShapeDtypeStruct((DEVICES * MSG, LANES), F32),
-            jax.ShapeDtypeStruct((PAIR, PAIR), F32),
+            jax.ShapeDtypeStruct((PAIR + EXTRA, PAIR), F32),
         ),
         in_specs=[hbm, hbm, hbm],
         out_specs=(pl.BlockSpec(memory_space=pltpu.VMEM),) * 2,
@@ -100,7 +110,7 @@
             pltpu.SMEM((1, TILES), jnp.int32),
             pltpu.VMEM((QUARTERS, V, LANES), F32),
             pltpu.VMEM((V, LANES), F32),
-            pltpu.SemaphoreType.DMA((QUARTERS + 2,)),
+            pltpu.SemaphoreType.DMA((QUARTERS + 3,)),
         ],
         compiler_params=pltpu.CompilerParams(vmem_limit_bytes=16 * 1024 * 1024),
         name="pack",
@@ -148,7 +158,8 @@
     table_copy.start()
 
     def fetch(slot):
-        return pltpu.make_async_copy(int_hbm.at[slot], int_ref.at[slot - 1], sems.at[slot])
+        rows = pl.ds(EXTRA, PAIR - EXTRA) if slot == 1 else pl.ds(0, PAIR)
+        return pltpu.make_async_copy(int_hbm.at[slot, rows, :], int_ref.at[slot - 1, rows, :], sems.at[slot])
 
     fetch(1).start()
     core = lax.axis_index("col_1")
@@ -169,18 +180,9 @@
         return top[:, :DEVICES] + top[:, DEVICES:] + low
 
     pieces = [slice(first, first + PIECE) for first in range(0, PAIR, PIECE)]
+    fetch(2).start()
+    fetch(3).start()
     prepare(0)
-    table_copy.wait()
-    own = lax.axis_index(ROW_COL)
-    count = jnp.int32(0)
-    for s in range(SLOTS):
-        count += (table_ref[s, 0, own] >= 0).astype(jnp.int32)
-    for slot in range(2, SLOTS):
-
-        @pl.when(slot < count)
-        def _():
-            fetch(slot).start()
-
     data = recv_ref[pl.ds(SLOTS * 8, DEVICES, stride=MSG), :]
     blocks = exchange_chunks([data[i * TB : (i + 1) * TB] for i in range(4)])
     left_high, left_low = split_parts(jnp.concatenate(blocks, axis=0).T)
@@ -197,21 +199,22 @@
                 turned_ref[pl.ds(half * (HALF * 8) + row, 8), :] = tiles[i * 8 : (i + 1) * 8]
 
     for rows in pieces:
-        acc_ref[rows, :] = jnp.where(count > 0, product(0, head_ref[rows, :]), 0.0)
-    fetch(1).wait()
-
-    def add_slot(slot, _):
+        acc_ref[rows, :] = product(0, head_ref[rows, :])
+    table_copy.wait()
+    own = lax.axis_index(ROW_COL)
+    count = jnp.int32(0)
+    for s in range(SLOTS):
+        count += (table_ref[s, 0, own] >= 0).astype(jnp.int32)
+    for rows in pieces:
+        acc_ref[rows, :] = jnp.where(count > 0, acc_ref[rows, :], 0.0)
+    for slot in range(1, SLOTS):
         prepare(slot)
-
-        @pl.when(slot > 1)
-        def _():
-            fetch(slot).wait()
-
+        fetch(slot).wait()
         for rows in pieces:
-            acc_ref[rows, :] += product(slot, int_ref[slot - 1, rows, :])
-        return 0
-
-    lax.fori_loop(1, count, add_slot, 0)
+            early = slot == 1 and rows.start < EXTRA
+            values = head_ref[PAIR + rows.start : PAIR + rows.stop, :] if early else int_ref[slot - 1, rows, :]
+            term = product(slot, values)
+            acc_ref[rows, :] += jnp.where(count > slot, term, 0.0)
     for m in range(8):
         ladder = acc_ref[m * LANES : (m + 1) * LANES, :].T
         for half, out_ref in enumerate((own_ref, other_ref)):

time: 69.4 us -> 70.1 us (1.010)
  Pallas kernels: 8.19 us -> 9.94 us
  starting transfers between devices: 1.05 us -> 0.09 us
  blocking collectives: 58.5 us -> 57.6 us
    pallas_call x1, Pallas kernels: 5.47 us -> 7.01 us  [partial_residual(): pl.pallas_call(main_kernel, out_shape=(jax.ShapeDtypeStruct((HALF * 8, LA...]
    ppermute x1, starting transfers between devices: 1.05 us -> 0.09 us  [body(): arrived = lax.ppermute(other, 'col_1', [(0, 1), (1, 0)])]
    all_to_all x1, blocking collectives: 16.4 us -> 15.6 us  [body(): lax.all_to_all(chip, ROW_COL[:3], split_axis=0, concat_axis=0, tiled=True)]
where the time goes in v5:
time: 70.1 us; the launch traced here: 69.9 us
  blocking collectives  57.6 us (82%)
  Pallas kernels  9.94 us (14%)
  waiting for transfers between devices  1.52 us (2%)
    all_to_all x1, blocking collectives, body(): lax.all_to_all(outgoing.reshape(DEVICES, MSG, 1, LANES), ROW_COL, split_a...  42 us
    all_to_all x1, blocking collectives, body(): lax.all_to_all(chip, ROW_COL[:3], split_axis=0, concat_axis=0, tiled=True)  15.6 us
    pallas_call x1, Pallas kernels, partial_residual(): pl.pallas_call(main_kernel, out_shape=(jax.ShapeDtypeStruct((HALF * 8, LA...  7.01 us
    pallas_call x1, Pallas kernels, pack(): pl.pallas_call(pack_kernel, out_shape=(jax.ShapeDtypeStruct((DEVICES * MS...  2.93 us
    ppermute x1, waiting for transfers between devices, body(): arrived = lax.ppermute(other, 'col_1', [(0, 1), (1, 0)])  1.52 us
  transfers between devices with their start and end apart: 1, of which 1 were waited for; matrix products, arithmetic and copies ran while one was open for 0% of the time, Pallas kernels for 0%

profile of v5, /device:TPU:0, one launch (start us, length us, event | category | flops | bytes accessed | tf_op | source)
XLA Modules:
  0.0 69.9 jit_solution(10660671645644881733)
XLA Ops:
  0.0 0.0 copy-start
  0.0 2.9 %pack.1 = (f32[4224,128]{1,0:T(8,128)S(1)}, f32[1280,1024]{1,0:T(8,128)S(1)}) custom-call(s32[4,2,128]{2,1,0:T(2,128)} %bitcast.12, f32[512,512]{1,0:T(8,128)} %bitcast.11, f32[4,1024,1024]{2,1,0:T(8,128)} %int_hbm.3), custom_call_target="tpu_custom_call" | custom-call | tf_op jit(solution)/shard_map/pack/pallas_call | solution.py:99
  2.9 42.0 %all_to_all.10 = f32[128,33,1,128]{3,2,1,0:T(1,128)S(1)} all-to-all(f32[128,33,1,128]{3,2,1,0:T(1,128)S(1)} %bitcast.9), channel_id=1, replica_groups=mesh['row_0'=4,'row_1'=4,'col_0'=4,'col_1'=2] {'row_0','row_1','col_0','..., dimensions={0} | all-to-all | bytes 4325376 | tf_op jit(solution)/shard_map/all_to_all | solution.py:256
  45.0 0.0 copy-done
  45.0 7.0 %residual.1 = (f32[512,128]{1,0:T(8,128)S(1)}, f32[512,128]{1,0:T(8,128)S(1)}) custom-call(s32[4,2,128]{2,1,0:T(2,128)} %bitcast.13, f32[4224,128]{1,0:T(8,128)S(1)} %bitcast.8, f32[1280,1024]{1,0:T(8,128)S(1)} %get-tuple-element.10.head_ref, f32[4,1024,1024]{2,1,0:T(8,128)} %int_hbm.3, f32[128,1024]{1,0:T(8,128)S(1)} %bitcast.10), custom_call_target="tpu_custom_call" | custom-call | tf_op jit(solution)/shard_map/residual/pallas_call | solution.py:228
  52.0 0.1 collective-permute-start
  52.1 1.5 %collective-permute-done = f32[512,128]{1,0:T(8,128)S(1)} collective-permute-done((f32[512,128]{1,0:T(8,128)S(1)}, f32[512,128]{1,0:T(8,128)S(1)}, u32[]{:S(2)}, u32[]{:S(2)}) %collective-permute-start) | collective-permute-done | bytes 262176 | tf_op jit(solution)/shard_map/ppermute | solution.py:260
  53.7 15.6 %all_to_all.11 = f32[64,8,128]{2,1,0:T(8,128)S(1)} all-to-all(f32[64,8,128]{2,1,0:T(8,128)S(1)} %add_bitcast_fusion), channel_id=1, replica_groups=mesh['row_0'=4,'row_1'=4,'col_0'=4,'col_1'=2] {'row_0','row_1','col_0'}, dimensions={0} | all-to-all | bytes 524288 | tf_op jit(solution)/shard_map/all_to_all | solution.py:262
  69.3 0.7 reduce_sum.9
  (1 shorter events, 0.0 us)
Async XLA Ops:
  0.0 45.0 %copy-start = (f32[4,32,1024]{2,1,0:T(8,128)S(1)}, f32[4,32,1024]{2,1,0:T(8,128)}, u32[]{:S(2)}) copy-start(f32[4,32,1024]{2,1,0:T(8,128)} %param.6) | copy-start | bytes 1572868
  52.0 1.6 %collective-permute-start = (f32[512,128]{1,0:T(8,128)S(1)}, f32[512,128]{1,0:T(8,128)S(1)}, u32[]{:S(2)}, u32[]{:S(2)}) collective-permute-start(f32[512,128]{1,0:T(8,128)S(1)} %get-tuple-element.12), channel_id=1, source_target_pairs={{0,1},{1,0},{2,3},{3,2},{4,5},{5,4},{6,7},{7,6},{8,9},{9,8},{10,11... | collective-permute-start | bytes 786440 | tf_op jit(solution)/shard_map/ppermute | solution.py:260

commit v6 on v4

--- a/solution.py
+++ b/solution.py
@@ -45,11 +45,13 @@
 
 
 def pack_kernel(
-    table_hbm, amp_hbm, int_hbm, send_ref, head_ref, table_ref, row_ref, place_ref, amp_ref, turned_ref, sems
+    table_hbm, amp_hbm, int_hbm, send_ref, head_ref, table_ref, row_ref, place_ref, first_ref, amp_ref, turned_ref, sems
 ):
     head_copy = pltpu.make_async_copy(int_hbm.at[0], head_ref, sems.at[QUARTERS + 1])
     table_copy = pltpu.make_async_copy(table_hbm, table_ref, sems.at[QUARTERS])
     table_copy.start()
+    first_copy = pltpu.make_async_copy(amp_hbm.at[pl.ds(0, TB), :], first_ref, sems.at[QUARTERS + 2])
+    first_copy.start()
     copies = []
     for group in range(QUARTERS):
         lanes = pl.ds(group * LANES, LANES)
@@ -68,6 +70,12 @@
     row_ref[...] = (found[0:1] * MSG + found[1:2] * 8).astype(jnp.int32)
     row_copy = pltpu.make_async_copy(row_ref, place_ref, sems.at[QUARTERS])
     row_copy.start()
+    first_copy.wait()
+    for group in range(QUARTERS):
+        lanes = slice(group * LANES, (group + 1) * LANES)
+        turned_ref[lanes, 0:TB] = first_ref[:, lanes].T
+    parts = [turned_ref[pl.ds(k, DEVICES, stride=4), :] for k in range(4)]
+    send_ref[pl.ds(SLOTS * 8, DEVICES, stride=MSG), :] = exchange_chunks(parts)[0]
     copies[0].wait()
     row_copy.wait()
     for group in range(QUARTERS):
@@ -78,9 +86,6 @@
             for upper in range(NVT):
                 row = place_ref[0, upper * NVT + group * 4 + h]
                 send_ref[pl.ds(row, 8), :] = tiles[upper * 8 : (upper + 1) * 8]
-        turned_ref[pl.ds(group * LANES, LANES), 0:TB] = amp_ref[group, 0:TB, :].T
-    parts = [turned_ref[pl.ds(k, DEVICES, stride=4), :] for k in range(4)]
-    send_ref[pl.ds(SLOTS * 8, DEVICES, stride=MSG), :] = exchange_chunks(parts)[0]
     head_copy.wait()
 
 
@@ -98,9 +103,10 @@
             pltpu.VMEM((SLOTS, 2, DEVICES), jnp.int32),
             pltpu.VMEM((1, TILES), jnp.int32),
             pltpu.SMEM((1, TILES), jnp.int32),
+            pltpu.VMEM((TB, V), F32),
             pltpu.VMEM((QUARTERS, V, LANES), F32),
             pltpu.VMEM((V, LANES), F32),
-            pltpu.SemaphoreType.DMA((QUARTERS + 2,)),
+            pltpu.SemaphoreType.DMA((QUARTERS + 3,)),
         ],
         compiler_params=pltpu.CompilerParams(vmem_limit_bytes=16 * 1024 * 1024),
         name="pack",
@@ -169,18 +175,9 @@
         return top[:, :DEVICES] + top[:, DEVICES:] + low
 
     pieces = [slice(first, first + PIECE) for first in range(0, PAIR, PIECE)]
+    fetch(2).start()
+    fetch(3).start()
     prepare(0)
-    table_copy.wait()
-    own = lax.axis_index(ROW_COL)
-    count = jnp.int32(0)
-    for s in range(SLOTS):
-        count += (table_ref[s, 0, own] >= 0).astype(jnp.int32)
-    for slot in range(2, SLOTS):
-
-        @pl.when(slot < count)
-        def _():
-            fetch(slot).start()
-
     data = recv_ref[pl.ds(SLOTS * 8, DEVICES, stride=MSG), :]
     blocks = exchange_chunks([data[i * TB : (i + 1) * TB] for i in range(4)])
     left_high, left_low = split_parts(jnp.concatenate(blocks, axis=0).T)
@@ -197,21 +194,41 @@
                 turned_ref[pl.ds(half * (HALF * 8) + row, 8), :] = tiles[i * 8 : (i + 1) * 8]
 
     for rows in pieces:
-        acc_ref[rows, :] = jnp.where(count > 0, product(0, head_ref[rows, :]), 0.0)
+        acc_ref[rows, :] = product(0, head_ref[rows, :])
+    table_copy.wait()
+    own = lax.axis_index(ROW_COL)
+    count = jnp.int32(0)
+    for s in range(SLOTS):
+        count += (table_ref[s, 0, own] >= 0).astype(jnp.int32)
+
+    @pl.when(count == 0)
+    def _():
+        acc_ref[...] = jnp.zeros_like(acc_ref)
+
     fetch(1).wait()
 
-    def add_slot(slot, _):
-        prepare(slot)
-
-        @pl.when(slot > 1)
-        def _():
-            fetch(slot).wait()
-
+    @pl.when(count > 1)
+    def _():
+        prepare(1)
         for rows in pieces:
-            acc_ref[rows, :] += product(slot, int_ref[slot - 1, rows, :])
-        return 0
-
-    lax.fori_loop(1, count, add_slot, 0)
+            acc_ref[rows, :] += product(1, int_ref[1 - 1, rows, :])
+
+    fetch(2).wait()
+
+    @pl.when(count > 2)
+    def _():
+        prepare(2)
+        for rows in pieces:
+            acc_ref[rows, :] += product(2, int_ref[2 - 1, rows, :])
+
+    fetch(3).wait()
+
+    @pl.when(count > 3)
+    def _():
+        prepare(3)
+        for rows in pieces:
+            acc_ref[rows, :] += product(3, int_ref[3 - 1, rows, :])
+
     for m in range(8):
         ladder = acc_ref[m * LANES : (m + 1) * LANES, :].T
         for half, out_ref in enumerate((own_ref, other_ref)):

time: 69.4 us -> 69.9 us (level)
  starting transfers between devices: 1.05 us -> 0.09 us
  Pallas kernels: 8.19 us -> 9.1 us
    pallas_call x1, Pallas kernels: 5.47 us -> 6.46 us  [partial_residual(): pl.pallas_call(main_kernel, out_shape=(jax.ShapeDtypeStruct((HALF * 8, LA...]
    ppermute x1, starting transfers between devices: 1.05 us -> 0.09 us  [body(): arrived = lax.ppermute(other, 'col_1', [(0, 1), (1, 0)])]
where the time goes in v6:
time: 69.9 us; the launch traced here: 69.6 us
  blocking collectives  58.1 us (83%)
  Pallas kernels  9.1 us (13%)
  waiting for transfers between devices  1.52 us (2%)
  other arithmetic  0.7 us (1%)
    all_to_all x1, blocking collectives, body(): lax.all_to_all(outgoing.reshape(DEVICES, MSG, 1, LANES), ROW_COL, split_a...  42 us
    all_to_all x1, blocking collectives, body(): lax.all_to_all(chip, ROW_COL[:3], split_axis=0, concat_axis=0, tiled=True)  16.1 us
    pallas_call x1, Pallas kernels, partial_residual(): pl.pallas_call(main_kernel, out_shape=(jax.ShapeDtypeStruct((HALF * 8, LA...  6.46 us
    pallas_call x1, Pallas kernels, pack(): pl.pallas_call(pack_kernel, out_shape=(jax.ShapeDtypeStruct((DEVICES * MS...  2.63 us
    ppermute x1, waiting for transfers between devices, body(): arrived = lax.ppermute(other, 'col_1', [(0, 1), (1, 0)])  1.52 us
  transfers between devices with their start and end apart: 1, of which 1 were waited for; matrix products, arithmetic and copies ran while one was open for 0% of the time, Pallas kernels for 0%

profile of v6, /device:TPU:0, one launch (start us, length us, event | category | flops | bytes accessed | tf_op | source)
XLA Modules:
  0.0 69.6 jit_solution(3334095148831042363)
XLA Ops:
  0.0 2.6 %pack.1 = (f32[4224,128]{1,0:T(8,128)S(1)}, f32[1024,1024]{1,0:T(8,128)S(1)}) custom-call(s32[4,2,128]{2,1,0:T(2,128)} %bitcast.12, f32[512,512]{1,0:T(8,128)} %bitcast.11, f32[4,1024,1024]{2,1,0:T(8,128)} %int_hbm.3), custom_call_target="tpu_custom_call" | custom-call | tf_op jit(solution)/shard_map/pack/pallas_call | solution.py:94
  2.6 0.0 copy-start
  2.7 42.0 %all_to_all.10 = f32[128,33,1,128]{3,2,1,0:T(1,128)S(1)} all-to-all(f32[128,33,1,128]{3,2,1,0:T(1,128)S(1)} %bitcast.9), channel_id=1, replica_groups=mesh['row_0'=4,'row_1'=4,'col_0'=4,'col_1'=2] {'row_0','row_1','col_0','..., dimensions={0} | all-to-all | bytes 4325376 | tf_op jit(solution)/shard_map/all_to_all | solution.py:270
  44.7 0.0 copy-done
  44.7 6.5 %residual.1 = (f32[512,128]{1,0:T(8,128)S(1)}, f32[512,128]{1,0:T(8,128)S(1)}) custom-call(s32[4,2,128]{2,1,0:T(2,128)} %bitcast.13, f32[4224,128]{1,0:T(8,128)S(1)} %bitcast.8, f32[1024,1024]{1,0:T(8,128)S(1)} %get-tuple-element.10.head_ref, f32[4,1024,1024]{2,1,0:T(8,128)} %int_hbm.3, f32[128,1024]{1,0:T(8,128)S(1)} %bitcast.10), custom_call_target="tpu_custom_call" | custom-call | tf_op jit(solution)/shard_map/residual/pallas_call | solution.py:242
  51.2 0.1 collective-permute-start
  51.3 1.5 %collective-permute-done = f32[512,128]{1,0:T(8,128)S(1)} collective-permute-done((f32[512,128]{1,0:T(8,128)S(1)}, f32[512,128]{1,0:T(8,128)S(1)}, u32[]{:S(2)}, u32[]{:S(2)}) %collective-permute-start) | collective-permute-done | bytes 262176 | tf_op jit(solution)/shard_map/ppermute | solution.py:274
  52.8 16.1 %all_to_all.11 = f32[64,8,128]{2,1,0:T(8,128)S(1)} all-to-all(f32[64,8,128]{2,1,0:T(8,128)S(1)} %add_bitcast_fusion), channel_id=1, replica_groups=mesh['row_0'=4,'row_1'=4,'col_0'=4,'col_1'=2] {'row_0','row_1','col_0'}, dimensions={0} | all-to-all | bytes 524288 | tf_op jit(solution)/shard_map/all_to_all | solution.py:276
  68.9 0.7 reduce_sum.9
  (1 shorter events, 0.0 us)
Async XLA Ops:
  2.6 42.1 %copy-start = (f32[4,32,1024]{2,1,0:T(8,128)S(1)}, f32[4,32,1024]{2,1,0:T(8,128)}, u32[]{:S(2)}) copy-start(f32[4,32,1024]{2,1,0:T(8,128)} %param.6) | copy-start | bytes 1572868
  51.2 1.6 %collective-permute-start = (f32[512,128]{1,0:T(8,128)S(1)}, f32[512,128]{1,0:T(8,128)S(1)}, u32[]{:S(2)}, u32[]{:S(2)}) collective-permute-start(f32[512,128]{1,0:T(8,128)S(1)} %get-tuple-element.12), channel_id=1, source_target_pairs={{0,1},{1,0},{2,3},{3,2},{4,5},{5,4},{6,7},{7,6},{8,9},{9,8},{10,11... | collective-permute-start | bytes 786440 | tf_op jit(solution)/shard_map/ppermute | solution.py:274

commit v7 on v4

--- a/solution.py
+++ b/solution.py
@@ -45,11 +45,13 @@
 
 
 def pack_kernel(
-    table_hbm, amp_hbm, int_hbm, send_ref, head_ref, table_ref, row_ref, place_ref, amp_ref, turned_ref, sems
+    table_hbm, amp_hbm, int_hbm, send_ref, head_ref, table_ref, row_ref, place_ref, first_ref, amp_ref, turned_ref, sems
 ):
     head_copy = pltpu.make_async_copy(int_hbm.at[0], head_ref, sems.at[QUARTERS + 1])
     table_copy = pltpu.make_async_copy(table_hbm, table_ref, sems.at[QUARTERS])
     table_copy.start()
+    first_copy = pltpu.make_async_copy(amp_hbm.at[pl.ds(0, TB), :], first_ref, sems.at[QUARTERS + 2])
+    first_copy.start()
     copies = []
     for group in range(QUARTERS):
         lanes = pl.ds(group * LANES, LANES)
@@ -68,6 +70,12 @@
     row_ref[...] = (found[0:1] * MSG + found[1:2] * 8).astype(jnp.int32)
     row_copy = pltpu.make_async_copy(row_ref, place_ref, sems.at[QUARTERS])
     row_copy.start()
+    first_copy.wait()
+    for group in range(QUARTERS):
+        lanes = slice(group * LANES, (group + 1) * LANES)
+        turned_ref[lanes, 0:TB] = first_ref[:, lanes].T
+    parts = [turned_ref[pl.ds(k, DEVICES, stride=4), :] for k in range(4)]
+    send_ref[pl.ds(SLOTS * 8, DEVICES, stride=MSG), :] = exchange_chunks(parts)[0]
     copies[0].wait()
     row_copy.wait()
     for group in range(QUARTERS):
@@ -78,9 +86,6 @@
             for upper in range(NVT):
                 row = place_ref[0, upper * NVT + group * 4 + h]
                 send_ref[pl.ds(row, 8), :] = tiles[upper * 8 : (upper + 1) * 8]
-        turned_ref[pl.ds(group * LANES, LANES), 0:TB] = amp_ref[group, 0:TB, :].T
-    parts = [turned_ref[pl.ds(k, DEVICES, stride=4), :] for k in range(4)]
-    send_ref[pl.ds(SLOTS * 8, DEVICES, stride=MSG), :] = exchange_chunks(parts)[0]
     head_copy.wait()
 
 
@@ -98,9 +103,10 @@
             pltpu.VMEM((SLOTS, 2, DEVICES), jnp.int32),
             pltpu.VMEM((1, TILES), jnp.int32),
             pltpu.SMEM((1, TILES), jnp.int32),
+            pltpu.VMEM((TB, V), F32),
             pltpu.VMEM((QUARTERS, V, LANES), F32),
             pltpu.VMEM((V, LANES), F32),
-            pltpu.SemaphoreType.DMA((QUARTERS + 2,)),
+            pltpu.SemaphoreType.DMA((QUARTERS + 3,)),
         ],
         compiler_params=pltpu.CompilerParams(vmem_limit_bytes=16 * 1024 * 1024),
         name="pack",

time: 69.4 us -> 69.1 us (level)
  starting transfers between devices: 1.05 us -> 0.09 us
    ppermute x1, starting transfers between devices: 1.05 us -> 0.09 us  [body(): arrived = lax.ppermute(other, 'col_1', [(0, 1), (1, 0)])]
where the time goes in v7:
time: 69.1 us; the launch traced here: 68.9 us
  blocking collectives  58.4 us (85%)
  Pallas kernels  8.11 us (12%)
  waiting for transfers between devices  1.52 us (2%)
  other arithmetic  0.7 us (1%)
    all_to_all x1, blocking collectives, body(): lax.all_to_all(outgoing.reshape(DEVICES, MSG, 1, LANES), ROW_COL, split_a...  42 us
    all_to_all x1, blocking collectives, body(): lax.all_to_all(chip, ROW_COL[:3], split_axis=0, concat_axis=0, tiled=True)  16.4 us
    pallas_call x1, Pallas kernels, partial_residual(): pl.pallas_call(main_kernel, out_shape=(jax.ShapeDtypeStruct((HALF * 8, LA...  5.48 us
    pallas_call x1, Pallas kernels, pack(): pl.pallas_call(pack_kernel, out_shape=(jax.ShapeDtypeStruct((DEVICES * MS...  2.63 us
    ppermute x1, waiting for transfers between devices, body(): arrived = lax.ppermute(other, 'col_1', [(0, 1), (1, 0)])  1.52 us
  transfers between devices with their start and end apart: 1, of which 1 were waited for; matrix products, arithmetic and copies ran while one was open for 0% of the time, Pallas kernels for 0%

profile of v7, /device:TPU:0, one launch (start us, length us, event | category | flops | bytes accessed | tf_op | source)
XLA Modules:
  0.0 68.9 jit_solution(15384088281651816508)
XLA Ops:
  0.0 2.6 %pack.1 = (f32[4224,128]{1,0:T(8,128)S(1)}, f32[1024,1024]{1,0:T(8,128)S(1)}) custom-call(s32[4,2,128]{2,1,0:T(2,128)} %bitcast.12, f32[512,512]{1,0:T(8,128)} %bitcast.11, f32[4,1024,1024]{2,1,0:T(8,128)} %int_hbm.3), custom_call_target="tpu_custom_call" | custom-call | tf_op jit(solution)/shard_map/pack/pallas_call | solution.py:94
  2.6 0.0 copy-start
  2.7 42.0 %all_to_all.10 = f32[128,33,1,128]{3,2,1,0:T(1,128)S(1)} all-to-all(f32[128,33,1,128]{3,2,1,0:T(1,128)S(1)} %bitcast.9), channel_id=1, replica_groups=mesh['row_0'=4,'row_1'=4,'col_0'=4,'col_1'=2] {'row_0','row_1','col_0','..., dimensions={0} | all-to-all | bytes 4325376 | tf_op jit(solution)/shard_map/all_to_all | solution.py:259
  44.7 0.0 copy-done
  44.7 5.5 %residual.1 = (f32[512,128]{1,0:T(8,128)S(1)}, f32[512,128]{1,0:T(8,128)S(1)}) custom-call(s32[4,2,128]{2,1,0:T(2,128)} %bitcast.13, f32[4224,128]{1,0:T(8,128)S(1)} %bitcast.8, f32[1024,1024]{1,0:T(8,128)S(1)} %get-tuple-element.10.head_ref, f32[4,1024,1024]{2,1,0:T(8,128)} %int_hbm.3, f32[128,1024]{1,0:T(8,128)S(1)} %bitcast.10), custom_call_target="tpu_custom_call" | custom-call | tf_op jit(solution)/shard_map/residual/pallas_call | solution.py:231
  50.2 0.1 collective-permute-start
  50.3 1.5 %collective-permute-done = f32[512,128]{1,0:T(8,128)S(1)} collective-permute-done((f32[512,128]{1,0:T(8,128)S(1)}, f32[512,128]{1,0:T(8,128)S(1)}, u32[]{:S(2)}, u32[]{:S(2)}) %collective-permute-start) | collective-permute-done | bytes 262176 | tf_op jit(solution)/shard_map/ppermute | solution.py:263
  51.8 16.4 %all_to_all.11 = f32[64,8,128]{2,1,0:T(8,128)S(1)} all-to-all(f32[64,8,128]{2,1,0:T(8,128)S(1)} %add_bitcast_fusion), channel_id=1, replica_groups=mesh['row_0'=4,'row_1'=4,'col_0'=4,'col_1'=2] {'row_0','row_1','col_0'}, dimensions={0} | all-to-all | bytes 524288 | tf_op jit(solution)/shard_map/all_to_all | solution.py:265
  68.2 0.7 reduce_sum.9
  (1 shorter events, 0.0 us)
Async XLA Ops:
  2.6 42.1 %copy-start = (f32[4,32,1024]{2,1,0:T(8,128)S(1)}, f32[4,32,1024]{2,1,0:T(8,128)}, u32[]{:S(2)}) copy-start(f32[4,32,1024]{2,1,0:T(8,128)} %param.6) | copy-start | bytes 1572868
  50.2 1.6 %collective-permute-start = (f32[512,128]{1,0:T(8,128)S(1)}, f32[512,128]{1,0:T(8,128)S(1)}, u32[]{:S(2)}, u32[]{:S(2)}) collective-permute-start(f32[512,128]{1,0:T(8,128)S(1)} %get-tuple-element.12), channel_id=1, source_target_pairs={{0,1},{1,0},{2,3},{3,2},{4,5},{5,4},{6,7},{7,6},{8,9},{9,8},{10,11... | collective-permute-start | bytes 786440 | tf_op jit(solution)/shard_map/ppermute | solution.py:263

commit v8 on v7

--- a/solution.py
+++ b/solution.py
@@ -181,11 +181,9 @@
     count = jnp.int32(0)
     for s in range(SLOTS):
         count += (table_ref[s, 0, own] >= 0).astype(jnp.int32)
-    for slot in range(2, SLOTS):
-
-        @pl.when(slot < count)
-        def _():
-            fetch(slot).start()
+    @pl.when(count > 2)
+    def _():
+        fetch(2).start()
 
     data = recv_ref[pl.ds(SLOTS * 8, DEVICES, stride=MSG), :]
     blocks = exchange_chunks([data[i * TB : (i + 1) * TB] for i in range(4)])
@@ -204,6 +202,10 @@
 
     for rows in pieces:
         acc_ref[rows, :] = jnp.where(count > 0, product(0, head_ref[rows, :]), 0.0)
+    @pl.when(count > 3)
+    def _():
+        fetch(3).start()
+
     fetch(1).wait()
 
     def add_slot(slot, _):

time: 69.1 us -> 68.9 us (level)
  Pallas kernels: 8.11 us -> 5.3 us
  blocking collectives: 58.4 us -> 60.9 us
  starting transfers between devices: 0.09 us -> 1.04 us
    pallas_call x1, Pallas kernels: 5.48 us -> 2.67 us  [partial_residual(): pl.pallas_call(main_kernel, out_shape=(jax.ShapeDtypeStruct((HALF * 8, LA...]
    all_to_all x1, blocking collectives: 16.4 us -> 18.8 us  [body(): lax.all_to_all(chip, ROW_COL[:3], split_axis=0, concat_axis=0, tiled=True)]
    ppermute x1, starting transfers between devices: 0.09 us -> 1.04 us  [body(): arrived = lax.ppermute(other, 'col_1', [(0, 1), (1, 0)])]
where the time goes in v8:
time: 68.9 us; the launch traced here: 69.1 us
  blocking collectives  60.9 us (88%)
  Pallas kernels  5.3 us (8%)
  waiting for transfers between devices  1.16 us (2%)
  starting transfers between devices  1.04 us (2%)
  other arithmetic  0.7 us (1%)
    all_to_all x1, blocking collectives, body(): lax.all_to_all(outgoing.reshape(DEVICES, MSG, 1, LANES), ROW_COL, split_a...  42 us
    all_to_all x1, blocking collectives, body(): lax.all_to_all(chip, ROW_COL[:3], split_axis=0, concat_axis=0, tiled=True)  18.8 us
    pallas_call x1, Pallas kernels, partial_residual(): pl.pallas_call(main_kernel, out_shape=(jax.ShapeDtypeStruct((HALF * 8, LA...  2.67 us
    pallas_call x1, Pallas kernels, pack(): pl.pallas_call(pack_kernel, out_shape=(jax.ShapeDtypeStruct((DEVICES * MS...  2.63 us
  transfers between devices with their start and end apart: 1, of which 1 were waited for; matrix products, arithmetic and copies ran while one was open for 0% of the time, Pallas kernels for 0%

profile of v8, /device:TPU:0, one launch (start us, length us, event | category | flops | bytes accessed | tf_op | source)
XLA Modules:
  0.0 69.1 jit_solution(15384088281651816508)
XLA Ops:
  0.0 2.6 %pack.1 = (f32[4224,128]{1,0:T(8,128)S(1)}, f32[1024,1024]{1,0:T(8,128)S(1)}) custom-call(s32[4,2,128]{2,1,0:T(2,128)} %bitcast.12, f32[512,512]{1,0:T(8,128)} %bitcast.11, f32[4,1024,1024]{2,1,0:T(8,128)} %int_hbm.3), custom_call_target="tpu_custom_call" | custom-call | tf_op jit(solution)/shard_map/pack/pallas_call | solution.py:94
  2.6 0.0 copy-start
  2.7 42.0 %all_to_all.10 = f32[128,33,1,128]{3,2,1,0:T(1,128)S(1)} all-to-all(f32[128,33,1,128]{3,2,1,0:T(1,128)S(1)} %bitcast.9), channel_id=1, replica_groups=mesh['row_0'=4,'row_1'=4,'col_0'=4,'col_1'=2] {'row_0','row_1','col_0','..., dimensions={0} | all-to-all | bytes 4325376 | tf_op jit(solution)/shard_map/all_to_all | solution.py:261
  44.7 0.0 copy-done
  44.7 2.7 %residual.1 = (f32[512,128]{1,0:T(8,128)S(1)}, f32[512,128]{1,0:T(8,128)S(1)}) custom-call(s32[4,2,128]{2,1,0:T(2,128)} %bitcast.13, f32[4224,128]{1,0:T(8,128)S(1)} %bitcast.8, f32[1024,1024]{1,0:T(8,128)S(1)} %get-tuple-element.10.head_ref, f32[4,1024,1024]{2,1,0:T(8,128)} %int_hbm.3, f32[128,1024]{1,0:T(8,128)S(1)} %bitcast.10), custom_call_target="tpu_custom_call" | custom-call | tf_op jit(solution)/shard_map/residual/pallas_call | solution.py:233
  47.4 1.0 %collective-permute-start = (f32[512,128]{1,0:T(8,128)S(1)}, f32[512,128]{1,0:T(8,128)S(1)}, u32[]{:S(2)}, u32[]{:S(2)}) collective-permute-start(f32[512,128]{1,0:T(8,128)S(1)} %get-tuple-element.12), channel_id=1, source_target_pairs={{0,1},{1,0},{2,3},{3,2},{4,5},{5,4},{6,7},{7,6},{8,9},{9,8},{10,11... | collective-permute-start | bytes 786440 | tf_op jit(solution)/shard_map/ppermute | solution.py:265
  48.4 1.2 %collective-permute-done = f32[512,128]{1,0:T(8,128)S(1)} collective-permute-done((f32[512,128]{1,0:T(8,128)S(1)}, f32[512,128]{1,0:T(8,128)S(1)}, u32[]{:S(2)}, u32[]{:S(2)}) %collective-permute-start) | collective-permute-done | bytes 262176 | tf_op jit(solution)/shard_map/ppermute | solution.py:265
  49.6 18.8 %all_to_all.11 = f32[64,8,128]{2,1,0:T(8,128)S(1)} all-to-all(f32[64,8,128]{2,1,0:T(8,128)S(1)} %add_bitcast_fusion), channel_id=1, replica_groups=mesh['row_0'=4,'row_1'=4,'col_0'=4,'col_1'=2] {'row_0','row_1','col_0'}, dimensions={0} | all-to-all | bytes 524288 | tf_op jit(solution)/shard_map/all_to_all | solution.py:267
  68.5 0.7 reduce_sum.9
  (1 shorter events, 0.0 us)
Async XLA Ops:
  2.6 42.1 %copy-start = (f32[4,32,1024]{2,1,0:T(8,128)S(1)}, f32[4,32,1024]{2,1,0:T(8,128)}, u32[]{:S(2)}) copy-start(f32[4,32,1024]{2,1,0:T(8,128)} %param.6) | copy-start | bytes 1572868
  47.4 2.2 %collective-permute-start = (f32[512,128]{1,0:T(8,128)S(1)}, f32[512,128]{1,0:T(8,128)S(1)}, u32[]{:S(2)}, u32[]{:S(2)}) collective-permute-start(f32[512,128]{1,0:T(8,128)S(1)} %get-tuple-element.12), channel_id=1, source_target_pairs={{0,1},{1,0},{2,3},{3,2},{4,5},{5,4},{6,7},{7,6},{8,9},{9,8},{10,11... | collective-permute-start | bytes 786440 | tf_op jit(solution)/shard_map/ppermute | solution.py:265

commit v9 on v7

--- a/solution.py
+++ b/solution.py
@@ -175,7 +175,8 @@
         return top[:, :DEVICES] + top[:, DEVICES:] + low
 
     pieces = [slice(first, first + PIECE) for first in range(0, PAIR, PIECE)]
-    prepare(0)
+    for slot in range(SLOTS):
+        prepare(slot)
     table_copy.wait()
     own = lax.axis_index(ROW_COL)
     count = jnp.int32(0)
@@ -207,8 +208,6 @@
     fetch(1).wait()
 
     def add_slot(slot, _):
-        prepare(slot)
-
         @pl.when(slot > 1)
         def _():
             fetch(slot).wait()

time: 69.1 us -> 68.6 us (level)
  blocking collectives: 58.4 us -> 57 us
  Pallas kernels: 8.11 us -> 9.3 us
    all_to_all x1, blocking collectives: 16.4 us -> 15 us  [body(): lax.all_to_all(chip, ROW_COL[:3], split_axis=0, concat_axis=0, tiled=True)]
    pallas_call x1, Pallas kernels: 5.48 us -> 6.66 us  [partial_residual(): pl.pallas_call(main_kernel, out_shape=(jax.ShapeDtypeStruct((HALF * 8, LA...]
where the time goes in v9:
time: 68.6 us; the launch traced here: 68.7 us
  blocking collectives  57 us (83%)
  Pallas kernels  9.3 us (14%)
  waiting for transfers between devices  1.52 us (2%)
  other arithmetic  0.7 us (1%)
    all_to_all x1, blocking collectives, body(): lax.all_to_all(outgoing.reshape(DEVICES, MSG, 1, LANES), ROW_COL, split_a...  42 us
    all_to_all x1, blocking collectives, body(): lax.all_to_all(chip, ROW_COL[:3], split_axis=0, concat_axis=0, tiled=True)  15 us
    pallas_call x1, Pallas kernels, partial_residual(): pl.pallas_call(main_kernel, out_shape=(jax.ShapeDtypeStruct((HALF * 8, LA...  6.66 us
    pallas_call x1, Pallas kernels, pack(): pl.pallas_call(pack_kernel, out_shape=(jax.ShapeDtypeStruct((DEVICES * MS...  2.63 us
    ppermute x1, waiting for transfers between devices, body(): arrived = lax.ppermute(other, 'col_1', [(0, 1), (1, 0)])  1.52 us
  transfers between devices with their start and end apart: 1, of which 1 were waited for; matrix products, arithmetic and copies ran while one was open for 0% of the time, Pallas kernels for 0%

profile of v9, /device:TPU:0, one launch (start us, length us, event | category | flops | bytes accessed | tf_op | source)
XLA Modules:
  0.0 68.7 jit_solution(1589178803202641384)
XLA Ops:
  0.0 2.6 %pack.1 = (f32[4224,128]{1,0:T(8,128)S(1)}, f32[1024,1024]{1,0:T(8,128)S(1)}) custom-call(s32[4,2,128]{2,1,0:T(2,128)} %bitcast.12, f32[512,512]{1,0:T(8,128)} %bitcast.11, f32[4,1024,1024]{2,1,0:T(8,128)} %int_hbm.3), custom_call_target="tpu_custom_call" | custom-call | tf_op jit(solution)/shard_map/pack/pallas_call | solution.py:94
  2.6 0.0 copy-start
  2.7 42.0 %all_to_all.10 = f32[128,33,1,128]{3,2,1,0:T(1,128)S(1)} all-to-all(f32[128,33,1,128]{3,2,1,0:T(1,128)S(1)} %bitcast.9), channel_id=1, replica_groups=mesh['row_0'=4,'row_1'=4,'col_0'=4,'col_1'=2] {'row_0','row_1','col_0','..., dimensions={0} | all-to-all | bytes 4325376 | tf_op jit(solution)/shard_map/all_to_all | solution.py:258
  44.7 0.0 copy-done
  44.7 6.7 %residual.1 = (f32[512,128]{1,0:T(8,128)S(1)}, f32[512,128]{1,0:T(8,128)S(1)}) custom-call(s32[4,2,128]{2,1,0:T(2,128)} %bitcast.13, f32[4224,128]{1,0:T(8,128)S(1)} %bitcast.8, f32[1024,1024]{1,0:T(8,128)S(1)} %get-tuple-element.10.head_ref, f32[4,1024,1024]{2,1,0:T(8,128)} %int_hbm.3, f32[128,1024]{1,0:T(8,128)S(1)} %bitcast.10), custom_call_target="tpu_custom_call" | custom-call | tf_op jit(solution)/shard_map/residual/pallas_call | solution.py:230
  51.4 0.1 collective-permute-start
  51.5 1.5 %collective-permute-done = f32[512,128]{1,0:T(8,128)S(1)} collective-permute-done((f32[512,128]{1,0:T(8,128)S(1)}, f32[512,128]{1,0:T(8,128)S(1)}, u32[]{:S(2)}, u32[]{:S(2)}) %collective-permute-start) | collective-permute-done | bytes 262176 | tf_op jit(solution)/shard_map/ppermute | solution.py:262
  53.0 15.0 %all_to_all.11 = f32[64,8,128]{2,1,0:T(8,128)S(1)} all-to-all(f32[64,8,128]{2,1,0:T(8,128)S(1)} %add_bitcast_fusion), channel_id=1, replica_groups=mesh['row_0'=4,'row_1'=4,'col_0'=4,'col_1'=2] {'row_0','row_1','col_0'}, dimensions={0} | all-to-all | bytes 524288 | tf_op jit(solution)/shard_map/all_to_all | solution.py:264
  68.0 0.7 reduce_sum.9
  (1 shorter events, 0.0 us)
Async XLA Ops:
  2.6 42.1 %copy-start = (f32[4,32,1024]{2,1,0:T(8,128)S(1)}, f32[4,32,1024]{2,1,0:T(8,128)}, u32[]{:S(2)}) copy-start(f32[4,32,1024]{2,1,0:T(8,128)} %param.6) | copy-start | bytes 1572868
  51.4 1.6 %collective-permute-start = (f32[512,128]{1,0:T(8,128)S(1)}, f32[512,128]{1,0:T(8,128)S(1)}, u32[]{:S(2)}, u32[]{:S(2)}) collective-permute-start(f32[512,128]{1,0:T(8,128)S(1)} %get-tuple-element.12), channel_id=1, source_target_pairs={{0,1},{1,0},{2,3},{3,2},{4,5},{5,4},{6,7},{7,6},{8,9},{9,8},{10,11... | collective-permute-start | bytes 786440 | tf_op jit(solution)/shard_map/ppermute | solution.py:262

commit v10 on v9

--- a/solution.py
+++ b/solution.py
@@ -207,16 +207,15 @@
         acc_ref[rows, :] = jnp.where(count > 0, product(0, head_ref[rows, :]), 0.0)
     fetch(1).wait()
 
-    def add_slot(slot, _):
-        @pl.when(slot > 1)
+    for slot in range(1, SLOTS):
+
+        @pl.when(slot < count)
         def _():
-            fetch(slot).wait()
-
-        for rows in pieces:
-            acc_ref[rows, :] += product(slot, int_ref[slot - 1, rows, :])
-        return 0
-
-    lax.fori_loop(1, count, add_slot, 0)
+            if slot > 1:
+                fetch(slot).wait()
+            for rows in pieces:
+                acc_ref[rows, :] += product(slot, int_ref[slot - 1, rows, :])
+
     for m in range(8):
         ladder = acc_ref[m * LANES : (m + 1) * LANES, :].T
         for half, out_ref in enumerate((own_ref, other_ref)):

time: 68.6 us -> 69.5 us (1.013)
  blocking collectives: 57 us -> 60.4 us
  Pallas kernels: 9.3 us -> 6.57 us
    all_to_all x1, blocking collectives: 15 us -> 18.3 us  [body(): lax.all_to_all(chip, ROW_COL[:3], split_axis=0, concat_axis=0, tiled=True)]
    pallas_call x1, Pallas kernels: 6.66 us -> 3.94 us  [partial_residual(): pl.pallas_call(main_kernel, out_shape=(jax.ShapeDtypeStruct((HALF * 8, LA...]
where the time goes in v10:
time: 69.5 us; the launch traced here: 69.3 us
  blocking collectives  60.4 us (87%)
  Pallas kernels  6.57 us (9%)
  waiting for transfers between devices  1.52 us (2%)
  other arithmetic  0.7 us (1%)
    all_to_all x1, blocking collectives, body(): lax.all_to_all(outgoing.reshape(DEVICES, MSG, 1, LANES), ROW_COL, split_a...  42 us
    all_to_all x1, blocking collectives, body(): lax.all_to_all(chip, ROW_COL[:3], split_axis=0, concat_axis=0, tiled=True)  18.3 us
    pallas_call x1, Pallas kernels, partial_residual(): pl.pallas_call(main_kernel, out_shape=(jax.ShapeDtypeStruct((HALF * 8, LA...  3.94 us
    pallas_call x1, Pallas kernels, pack(): pl.pallas_call(pack_kernel, out_shape=(jax.ShapeDtypeStruct((DEVICES * MS...  2.63 us
    ppermute x1, waiting for transfers between devices, body(): arrived = lax.ppermute(other, 'col_1', [(0, 1), (1, 0)])  1.52 us
  transfers between devices with their start and end apart: 1, of which 1 were waited for; matrix products, arithmetic and copies ran while one was open for 0% of the time, Pallas kernels for 0%

profile of v10, /device:TPU:0, one launch (start us, length us, event | category | flops | bytes accessed | tf_op | source)
XLA Modules:
  0.0 69.3 jit_solution(4552750937937118363)
XLA Ops:
  0.0 2.6 %pack.1 = (f32[4224,128]{1,0:T(8,128)S(1)}, f32[1024,1024]{1,0:T(8,128)S(1)}) custom-call(s32[4,2,128]{2,1,0:T(2,128)} %bitcast.12, f32[512,512]{1,0:T(8,128)} %bitcast.11, f32[4,1024,1024]{2,1,0:T(8,128)} %int_hbm.3), custom_call_target="tpu_custom_call" | custom-call | tf_op jit(solution)/shard_map/pack/pallas_call | solution.py:94
  2.6 0.0 copy-start
  2.7 42.0 %all_to_all.10 = f32[128,33,1,128]{3,2,1,0:T(1,128)S(1)} all-to-all(f32[128,33,1,128]{3,2,1,0:T(1,128)S(1)} %bitcast.9), channel_id=1, replica_groups=mesh['row_0'=4,'row_1'=4,'col_0'=4,'col_1'=2] {'row_0','row_1','col_0','..., dimensions={0} | all-to-all | bytes 4325376 | tf_op jit(solution)/shard_map/all_to_all | solution.py:257
  44.7 0.0 copy-done
  44.7 3.9 %residual.1 = (f32[512,128]{1,0:T(8,128)S(1)}, f32[512,128]{1,0:T(8,128)S(1)}) custom-call(s32[4,2,128]{2,1,0:T(2,128)} %bitcast.13, f32[4224,128]{1,0:T(8,128)S(1)} %bitcast.8, f32[1024,1024]{1,0:T(8,128)S(1)} %get-tuple-element.10.head_ref, f32[4,1024,1024]{2,1,0:T(8,128)} %int_hbm.3, f32[128,1024]{1,0:T(8,128)S(1)} %bitcast.10), custom_call_target="tpu_custom_call" | custom-call | tf_op jit(solution)/shard_map/residual/pallas_call | solution.py:229
  48.6 0.1 collective-permute-start
  48.7 1.5 %collective-permute-done = f32[512,128]{1,0:T(8,128)S(1)} collective-permute-done((f32[512,128]{1,0:T(8,128)S(1)}, f32[512,128]{1,0:T(8,128)S(1)}, u32[]{:S(2)}, u32[]{:S(2)}) %collective-permute-start) | collective-permute-done | bytes 262176 | tf_op jit(solution)/shard_map/ppermute | solution.py:261
  50.3 18.3 %all_to_all.11 = f32[64,8,128]{2,1,0:T(8,128)S(1)} all-to-all(f32[64,8,128]{2,1,0:T(8,128)S(1)} %add_bitcast_fusion), channel_id=1, replica_groups=mesh['row_0'=4,'row_1'=4,'col_0'=4,'col_1'=2] {'row_0','row_1','col_0'}, dimensions={0} | all-to-all | bytes 524288 | tf_op jit(solution)/shard_map/all_to_all | solution.py:263
  68.6 0.7 reduce_sum.9
  (1 shorter events, 0.0 us)
Async XLA Ops:
  2.6 42.1 %copy-start = (f32[4,32,1024]{2,1,0:T(8,128)S(1)}, f32[4,32,1024]{2,1,0:T(8,128)}, u32[]{:S(2)}) copy-start(f32[4,32,1024]{2,1,0:T(8,128)} %param.6) | copy-start | bytes 1572868
  48.6 1.6 %collective-permute-start = (f32[512,128]{1,0:T(8,128)S(1)}, f32[512,128]{1,0:T(8,128)S(1)}, u32[]{:S(2)}, u32[]{:S(2)}) collective-permute-start(f32[512,128]{1,0:T(8,128)S(1)} %get-tuple-element.12), channel_id=1, source_target_pairs={{0,1},{1,0},{2,3},{3,2},{4,5},{5,4},{6,7},{7,6},{8,9},{9,8},{10,11... | collective-permute-start | bytes 786440 | tf_op jit(solution)/shard_map/ppermute | solution.py:261
